TPU v7x, 256 devices: a whole 4x4x8 slice. The times are simulated.
256 devices in a mesh: dp: 16 (over z, x_hi), ctx: 16 (over x_lo, y, core).
Axes of the slice: x: 4 (x_hi: 2, x_lo: 2; x = x_hi * 2 + x_lo), y: 4, z: 8, core: 2. Of those that a mesh axis runs over, the one named last changes fastest.
Arguments:
- features: bfloat16 [16, 8192, 768], P('dp', 'ctx'), may hold values from -24 to 24
- bases: int32 [16, 8192], P('dp', 'ctx'), may hold values from 0 to 3
- dna_table: bfloat16 [4, 768], replicated, may hold values from -6 to 6
- norm_gain: bfloat16 [768], replicated, may hold values from 0.099609375 to 1.8984375
- w_conv: bfloat16 [5, 768, 768], replicated, may hold values from -0.09375 to 0.09375
- w_query: bfloat16 [768, 768], replicated, may hold values from -0.21875 to 0.21875
- w_key: bfloat16 [768, 768], replicated, may hold values from -0.21875 to 0.21875
- w_value: bfloat16 [768, 768], replicated, may hold values from -0.21875 to 0.21875
- w_out: bfloat16 [768, 768], replicated, may hold values from -0.21875 to 0.21875
- cotangent: bfloat16 [16, 512, 768], P('dp', 'ctx'), may hold values from -48 to 48
Outputs:
- grad_features: bfloat16 [16, 8192, 768], P('dp', 'ctx')
- grad_conv: float32 [768, 5, 768], P('ctx', None, 'dp')
All inputs are finite; a program needn't handle non-finite values.
Results may differ from a plain program's by a relative error of at most 0.025.
The roundings to bfloat16 on the way count: a program that leaves them out, or rounds other values in their place, can miss the bound.
Values may be sent and summed in bfloat16 or wider, within the bound.
A program may use at most 128 MiB of HBM per device.

v0:
```python
import jax
import jax.numpy as jnp
from jax import lax
from jax.sharding import PartitionSpec as P

HEADS = 6
DH = 128


EPSILON = 1e-06
GELU_SCALE = 0.7978845608028654
CUBIC = 0.044715


def extended(block, sides, width):
    for axis, dim in sides:
        count = lax.axis_size(axis)
        forward = [(i, i + 1) for i in range(count - 1)]
        backward = [(target, source) for source, target in forward]
        low = lax.ppermute(
            lax.slice_in_dim(block, block.shape[dim] - width, None, axis=dim), axis, forward
        )
        high = lax.ppermute(lax.slice_in_dim(block, 0, width, axis=dim), axis, backward)
        block = jnp.concatenate([low, block, high], axis=dim)
    return block


def gelu_pair(inputs):
    inner = GELU_SCALE * (inputs + CUBIC * inputs**3)
    tanh_val = jnp.tanh(inner)
    values = 0.5 * inputs * (1.0 + tanh_val)
    slopes = 0.5 * (1.0 + tanh_val) + 0.5 * inputs * (1.0 - tanh_val**2) * GELU_SCALE * (
        1.0 + 3.0 * CUBIC * inputs**2
    )
    return (values, slopes)


def heads_split(matrix):
    return matrix.reshape(matrix.shape[0], HEADS, DH)


def dot_right_t(left, right):
    return lax.dot_general(
        left, right, (((1,), (1,)), ((), ())), preferred_element_type=jnp.float32
    )


def dot_left_t(left, right):
    return lax.dot_general(
        left, right, (((0,), (0,)), ((), ())), preferred_element_type=jnp.float32
    )


def per_device(
    features, bases, dna_table, norm_gain, w_conv, w_query, w_key, w_value, w_out, cotangent
):
    seg_feat = features[0]
    seg_base = bases[0]
    seg_cot = cotangent[0]
    kernel = w_conv.shape[0]
    half_width = kernel // 2
    length = seg_feat.shape[0]
    channels = seg_feat.shape[1]
    tok_rows = seg_cot.shape[0]
    onehot = (seg_base[:, None] == jnp.arange(4, dtype=jnp.int32)[None, :]).astype(jnp.bfloat16)
    summed_in = seg_feat.astype(jnp.float32) + jnp.dot(
        onehot, dna_table, preferred_element_type=jnp.float32
    )
    inv_rms = lax.rsqrt(jnp.mean(summed_in * summed_in, axis=-1, keepdims=True) + EPSILON)
    normed = summed_in * inv_rms
    gain_f = norm_gain.astype(jnp.float32)
    pre_gelu = normed * gain_f
    gelu_val, slopes = gelu_pair(pre_gelu)
    act = gelu_val.astype(jnp.bfloat16)
    rimmed = extended(act[None], (("ctx", 1),), half_width)[0]
    conv = jnp.zeros((length, channels), jnp.float32)
    for offset in range(kernel):
        conv = conv + jnp.dot(
            rimmed[offset : offset + length], w_conv[offset], preferred_element_type=jnp.float32
        )
    resid = summed_in + conv
    pooled = resid.reshape(tok_rows, -1, channels).mean(axis=1).astype(jnp.bfloat16)
    queries = jnp.dot(pooled, w_query, preferred_element_type=jnp.float32).astype(jnp.bfloat16)
    keys_local = jnp.dot(pooled, w_key, preferred_element_type=jnp.float32).astype(jnp.bfloat16)
    values_local = jnp.dot(pooled, w_value, preferred_element_type=jnp.float32).astype(jnp.bfloat16)
    keys_all, values_all = (
        lax.all_gather(keys_local, "ctx", axis=0, tiled=True),
        lax.all_gather(values_local, "ctx", axis=0, tiled=True),
    )
    scale = 1.0 / DH**0.5
    query_heads = heads_split(queries)
    key_heads = heads_split(keys_all)
    value_heads = heads_split(values_all)
    scores = (
        jnp.einsum("qhd,khd->hqk", query_heads, key_heads, preferred_element_type=jnp.float32)
        * scale
    )
    row_max = jnp.max(scores, axis=-1, keepdims=True)
    expo = jnp.exp(scores - row_max)
    row_total = jnp.sum(expo, axis=-1, keepdims=True)
    probs = expo / row_total
    probs_b = probs.astype(jnp.bfloat16)
    attn_out = jnp.einsum("hqk,khd->qhd", probs_b, value_heads, preferred_element_type=jnp.float32)
    attn_out = attn_out.reshape(tok_rows, channels).astype(jnp.bfloat16)
    grad_attn = dot_right_t(seg_cot, w_out).astype(jnp.bfloat16)
    grad_heads = heads_split(grad_attn)
    grad_prob = jnp.einsum(
        "qhd,khd->hqk", grad_heads, value_heads, preferred_element_type=jnp.float32
    )
    delta_rows = jnp.sum(
        grad_heads.astype(jnp.float32) * heads_split(attn_out).astype(jnp.float32), axis=-1
    )
    row_delta = delta_rows.transpose(1, 0)[:, :, None]
    grad_score = (probs * (grad_prob - row_delta) * scale).astype(jnp.bfloat16)
    grad_q = jnp.einsum("hqk,khd->qhd", grad_score, key_heads, preferred_element_type=jnp.float32)
    grad_q = grad_q.reshape(tok_rows, channels).astype(jnp.bfloat16)
    term_k = jnp.einsum("hqk,qhd->khd", grad_score, query_heads, preferred_element_type=jnp.float32)
    term_v = jnp.einsum("hqk,qhd->khd", probs_b, grad_heads, preferred_element_type=jnp.float32)
    summed_kv = lax.psum_scatter(
        jnp.concatenate(
            (
                term_k.reshape(lax.axis_size("ctx") * tok_rows, channels),
                term_v.reshape(lax.axis_size("ctx") * tok_rows, channels),
            ),
            axis=1,
        ),
        "ctx",
        scatter_dimension=0,
        tiled=True,
    )
    grad_k = summed_kv[:, :channels].astype(jnp.bfloat16)
    grad_v = summed_kv[:, channels:].astype(jnp.bfloat16)
    grad_pooled = (
        seg_cot.astype(jnp.float32)
        + dot_right_t(grad_q, w_query)
        + dot_right_t(grad_k, w_key)
        + dot_right_t(grad_v, w_value)
    )
    pool_size = length // tok_rows
    grad_rows = jnp.repeat((grad_pooled / pool_size).astype(jnp.bfloat16), pool_size, axis=0)
    grad_pad = extended(grad_rows[None], (("ctx", 1),), half_width)[0]
    grad_act = jnp.zeros((length, channels), jnp.float32)
    for offset in range(kernel):
        begin = 2 * half_width - offset
        grad_act = grad_act + dot_right_t(grad_pad[begin : begin + length], w_conv[offset])
    windows = jnp.stack(
        [rimmed[offset : offset + length] for offset in range(kernel)], axis=2
    ).reshape(length, channels * kernel)
    factor = 1.0 / (lax.axis_size("dp") * length * lax.axis_size("ctx")) ** 0.5
    whole_terms = (dot_left_t(windows, grad_rows) * factor).reshape(channels, kernel, channels)
    shared = lax.psum_scatter(whole_terms, "ctx", scatter_dimension=0, tiled=True)
    grad_conv = lax.psum_scatter(shared, "dp", scatter_dimension=2, tiled=True)
    grad_norm = grad_act * slopes * gain_f
    grad_in = grad_rows.astype(jnp.float32) + inv_rms * (
        grad_norm - normed * jnp.mean(grad_norm * normed, axis=-1, keepdims=True)
    )
    return (grad_in.astype(jnp.bfloat16)[None], grad_conv)


def solution(mesh):
    in_specs = (
        P("dp", "ctx", None),
        P("dp", "ctx"),
        P(),
        P(),
        P(),
        P(),
        P(),
        P(),
        P(),
        P("dp", "ctx", None),
    )
    out_specs = (P("dp", "ctx", None), P("ctx", None, "dp"))
    return jax.shard_map(
        per_device, mesh=mesh, in_specs=in_specs, out_specs=out_specs, check_vma=False
    )
```

profile of v0, /device:TPU:1, one launch (start us, length us, event | category | flops | bytes accessed | tf_op | source)
XLA Modules:
  0.0 529.3 jit_solution(988875582411830763)
XLA Ops:
  7.2 0.0 reduce-scatter.10.cloned.1.call-start
  7.2 0.8 convert_element_type.74
  8.0 1.7 multiply_reduce_fusion.1
  9.7 0.7 fusion.122
  10.4 4.6 collective-permute-start
  15.0 2.3 collective-permute-start.1
  17.3 2.5 fusion.22
  19.8 1.1 fusion.40
  21.0 0.8 fusion.26
  21.8 0.8 fusion.30
  22.6 0.8 fusion.18
  23.4 1.1 bitcast_reduce_fusion
  24.5 0.9 fusion.39
  25.4 0.9 convolution_convert_fusion.2
  26.4 0.3 convolution_convert_fusion.5
  26.7 23.7 %all_gather.6 = bf16[512,768]{1,0:T(8,128)(2,1)} all-gather(bf16[32,768]{1,0:T(8,128)(2,1)S(1)} %convolution_convert_fusion.5), channel_id=1, replica_groups=mesh['dp'=16,'ctx'=16] {'ctx'}, dimensions={0}, use_global_device_ids=true | all-gather | bytes 835584 | tf_op jit(solution)/shard_map/all_gather | solution.py:87
  50.4 2.3 copy.36
  52.7 1.4 convolution_multiply_fusion.1
  54.1 0.8 copy-done.7
  54.9 0.9 fusion.100
  55.7 19.8 %all_gather.7 = bf16[512,768]{1,0:T(8,128)(2,1)} all-gather(bf16[32,768]{1,0:T(8,128)(2,1)S(1)} %copy-done.13), channel_id=1, replica_groups=mesh['dp'=16,'ctx'=16] {'ctx'}, dimensions={0}, use_global_device_ids=true | all-gather | bytes 835584 | tf_op jit(solution)/shard_map/all_gather | solution.py:88
  75.5 2.3 copy.39
  77.9 2.8 fusion.77
  80.7 2.4 fusion.38
  83.2 1.6 fusion.32
  84.8 0.7 copy-done.9
  85.5 0.4 fusion.80
  85.9 2.0 pad_maximum_fusion
  87.9 3.6 copy.54
  91.5 0.0 reduce-scatter.10.cloned.1.call-update
  91.5 0.2 reduce-scatter.8.cloned.1.call-start
  91.7 0.4 copy-done.15
  92.1 1.1 bitcast_dynamic-update-slice_fusion.4
  93.2 1.1 bitcast_dynamic-update-slice_fusion.3
  94.3 1.6 bitcast_dynamic-update-slice_fusion.2
  95.9 1.2 bitcast_dynamic-update-slice_fusion.1
  97.0 1.1 bitcast_dynamic-update-slice_fusion
  98.1 8.4 %copy.48 = bf16[512,768,5]{0,2,1:T(8,128)(2,1)} copy(bf16[512,768,5]{1,0,2:T(8,128)(2,1)} %bitcast_dynamic-update-slice_fusion) | data formatting | bytes 7864320 | tf_op jit(solution)/shard_map/stack | solution.py:146
  106.5 8.5 %reshape.82 = bf16[512,3840]{0,1:T(8,128)(2,1)} reshape(bf16[512,768,5]{0,2,1:T(8,128)(2,1)} %copy.48) | data formatting | bytes 7864320 | tf_op jit(solution)/shard_map/reshape | solution.py:148
  115.1 1.3 fusion.41
  116.4 1.3 convolution_add_fusion.2
  117.7 38.8 %reduce-scatter.10.cloned.1.call-done = f32[32,1536]{1,0:T(8,128)} async-done(((f32[512,1536]{1,0:T(8,128)}), f32[32,1536]{1,0:T(8,128)}) %reduce-scatter.10.cloned.1.call-update) | async-done | bytes 196624
  156.5 1.1 copy.55
  157.6 1.7 convolution_add_fusion.1
  159.4 0.0 copy-done.6
  159.4 0.5 fusion.34
  159.9 0.1 broadcast_in_dim.7
  159.9 9.7 %convolution_multiply_fusion = f32[3840,768]{1,0:T(8,128)} fusion(bf16[512,3840]{0,1:T(8,128)(2,1)} %reshape.82, bf16[512,768]{1,0:T(8,128)(2,1)S(1)} %bitcast.148), kind=kOutput, calls=%fused_computation.1 | convolution fusion | flops 3022848000 | bytes 16515072 | tf_op jit(solution)/shard_map/dot_general | solution.py:49
  169.7 14.8 %reshape.83 = f32[768,5,768]{2,1,0:T(8,128)} reshape(f32[3840,768]{1,0:T(8,128)} %convolution_multiply_fusion) | data formatting | bytes 23592960 | tf_op jit(solution)/shard_map/reshape | solution.py:150
  184.5 0.0 reduce-scatter.12.cloned.1.call-start
  184.6 6.1 %collective-permute-start.2 = (bf16[1,2,768]{2,1,0:T(2,128)(2,1)S(1)}, bf16[1,2,768]{2,1,0:T(2,128)(2,1)S(1)}, u32[]{:S(2)}, u32[]{:S(2)}) collective-permute-start(bf16[1,2,768]{2,1,0:T(2,128)(2,1)S(1)} %get-tuple-element.6), channel_id=1, source_target_pairs={{1,0},{2,1},{3,2},{4,3},{5,4},{6,5},{7,6},{8,7},{9,8},{10,9},{11,1... | collective-permute-start | bytes 9224 | tf_op jit(solution)/shard_map/ppermute | solution.py:23
  190.7 3.2 fusion.20
  193.9 2.1 collective-permute-start.3
  196.1 3.2 fusion.24
  199.3 97.3 %reduce-scatter.8.cloned.1.call-done = f32[48,5,768]{2,1,0:T(8,128)} async-done(((f32[768,5,768]{2,1,0:T(8,128)}), f32[48,5,768]{2,1,0:T(8,128)}) %reduce-scatter.8.cloned.1.call-update) | async-done | bytes 737296 | tf_op jit(solution)/shard_map/reduce_scatter | solution.py:151
  296.6 13.2 %copy.56 = f32[48,5,768]{1,0,2:T(8,128)} copy(f32[48,5,768]{2,1,0:T(8,128)} %reduce-scatter.8.cloned.1.call-done) | data formatting | bytes 1474560
  309.8 12.9 %reshape.87 = f32[768,240]{1,0:T(8,128)} reshape(f32[768,48,5]{2,1,0:T(8,128)} %bitcast.142) | data formatting | bytes 1474560
  322.7 2.1 fusion.28
  324.9 2.2 fusion.16
  327.1 3.3 multiply_reduce_fusion
  330.4 1.3 fusion.60
  331.7 188.5 %reduce-scatter.12.cloned.1.call-done = f32[48,240]{1,0:T(8,128)} async-done(((f32[768,240]{1,0:T(8,128)}), f32[48,240]{1,0:T(8,128)}) %reduce-scatter.12.cloned.1.call-update) | async-done | bytes 46096
  520.2 1.4 reshape.88
  521.6 1.2 copy.49
  (42 shorter events, 0.2 us)
Async XLA Ops:
  7.2 17.3 %copy-start = (bf16[768,768]{1,0:T(8,128)(2,1)S(1)}, bf16[768,768]{1,0:T(8,128)(2,1)}, u32[]{:S(2)}) copy-start(bf16[768,768]{1,0:T(8,128)(2,1)} %param.15) | copy-start | bytes 3538948
  7.2 149.3 %reduce-scatter.10.cloned.1.call-start = ((), (), s32[]{:S(2)}) async-start(), calls=%async_computation.4 | async-start | bytes 3342336
  10.4 10.6 %collective-permute-start = (bf16[1,2,768]{2,1,0:T(2,128)(2,1)S(1)}, bf16[1,2,768]{2,1,0:T(2,128)(2,1)S(1)}, u32[]{:S(2)}, u32[]{:S(2)}) collective-permute-start(bf16[1,2,768]{2,1,0:T(2,128)(2,1)S(1)} %get-tuple-element.8), channel_id=1, source_target_pairs={{0,1},{1,2},{2,3},{3,4},{4,5},{5,6},{6,7},{7,8},{8,9},{9,10},{10,1... | collective-permute-start | bytes 9224 | tf_op jit(solution)/shard_map/ppermute | solution.py:20
  15.0 4.9 copy-start.8
  15.0 4.9 copy-start.12
  15.0 6.0 %copy-start.11 = (bf16[5,768,768]{2,1,0:T(8,128)(2,1)S(1)}, bf16[5,768,768]{2,1,0:T(8,128)(2,1)}, u32[]{:S(2)}) copy-start(bf16[5,768,768]{2,1,0:T(8,128)(2,1)} %param.14) | copy-start | bytes 17694724
  15.0 7.6 %collective-permute-start.1 = (bf16[1,2,768]{2,1,0:T(2,128)(2,1)S(1)}, bf16[1,2,768]{2,1,0:T(2,128)(2,1)S(1)}, u32[]{:S(2)}, u32[]{:S(2)}) collective-permute-start(bf16[1,2,768]{2,1,0:T(2,128)(2,1)S(1)} %get-tuple-element.9), channel_id=1, source_target_pairs={{1,0},{2,1},{3,2},{4,3},{5,4},{6,5},{7,6},{8,7},{9,8},{10,9},{11,1... | collective-permute-start | bytes 9224 | tf_op jit(solution)/shard_map/ppermute | solution.py:23
  21.0 0.8 copy-start.14
  23.4 2.1 copy-start.5
  24.5 1.9 copy-start.4
  52.7 3.1 copy-start.13
  54.1 0.8 copy-start.7
  83.2 2.3 copy-start.10
  83.2 2.7 copy-start.3
  84.8 0.7 copy-start.9
  91.5 0.7 copy-start.15
  91.5 205.1 %reduce-scatter.8.cloned.1.call-start = ((), (), s32[]{:S(2)}) async-start(), calls=%async_computation.3 | async-start | bytes 20054016 | tf_op jit(solution)/shard_map/reduce_scatter | solution.py:151
  106.5 8.6 %copy-start.2 = (bf16[512,768]{0,1:T(8,128)(2,1)S(1)}, bf16[512,768]{0,1:T(8,128)(2,1)}, u32[]{:S(2)}) copy-start(bf16[512,768]{0,1:T(8,128)(2,1)} %copy.36) | copy-start | bytes 2359300
  117.7 41.7 %copy-start.6 = (bf16[768,768]{1,0:T(8,128)(2,1)S(1)}, bf16[768,768]{1,0:T(8,128)(2,1)}, u32[]{:S(2)}) copy-start(bf16[768,768]{1,0:T(8,128)(2,1)} %param.17) | copy-start | bytes 3538948
  184.5 335.7 %reduce-scatter.12.cloned.1.call-start = ((), (), s32[]{:S(2)}) async-start(), calls=%async_computation.5 | async-start | bytes 835584
  184.6 11.5 %collective-permute-start.2 = (bf16[1,2,768]{2,1,0:T(2,128)(2,1)S(1)}, bf16[1,2,768]{2,1,0:T(2,128)(2,1)S(1)}, u32[]{:S(2)}, u32[]{:S(2)}) collective-permute-start(bf16[1,2,768]{2,1,0:T(2,128)(2,1)S(1)} %get-tuple-element.6), channel_id=1, source_target_pairs={{1,0},{2,1},{3,2},{4,3},{5,4},{6,5},{7,6},{8,7},{9,8},{10,9},{11,1... | collective-permute-start | bytes 9224 | tf_op jit(solution)/shard_map/ppermute | solution.py:23
  193.9 130.9 %collective-permute-start.3 = (bf16[1,2,768]{2,1,0:T(2,128)(2,1)S(1)}, bf16[1,2,768]{2,1,0:T(2,128)(2,1)S(1)}, u32[]{:S(2)}, u32[]{:S(2)}) collective-permute-start(bf16[1,2,768]{2,1,0:T(2,128)(2,1)S(1)} %get-tuple-element.7), channel_id=1, source_target_pairs={{0,1},{1,2},{2,3},{3,4},{4,5},{5,6},{6,7},{7,8},{8,9},{9,10},{10,1... | collective-permute-start | bytes 9224 | tf_op jit(solution)/shard_map/ppermute | solution.py:20
  324.8 2.3 copy-start.16
  324.8 2.3 copy-start.17
  330.4 192.4 %copy-start.1 = (bf16[768,768]{1,0:T(8,128)(2,1)S(1)}, bf16[768,768]{1,0:T(8,128)(2,1)}, u32[]{:S(2)}) copy-start(bf16[768,768]{1,0:T(8,128)(2,1)} %param.15) | copy-start | bytes 3538948
Sparse Core Ops, SparseCore 0:
  91.6 64.8 reduce-scatter.9
  184.6 111.9 reduce-scatter.7
  322.9 197.3 reduce-scatter.11
where the time goes:
time: 536 us; the launch traced here: 529 us
  waiting for transfers between devices  325 us (61%)
  local copies, waits for them, and re-layouts  71.8 us (13%)
  matrix products  48.2 us (9%)
  blocking collectives  43.5 us (8%)
  starting transfers between devices  15.5 us (3%)
  between operations  14.1 us (3%)
  other arithmetic  11.5 us (2%)
    unnamed x5, waiting for transfers between devices  227 us
    reduce_scatter x1, waiting for transfers between devices, per_device(): lax.psum_scatter(whole_terms, 'ctx', scatter_dimension=0, tiled=True)  97.3 us
    unnamed x42, local copies, waits for them, and re-layouts  35.3 us
    all_gather x1, blocking collectives, per_device(): lax.all_gather(keys_local, 'ctx', axis=0, tiled=True)  23.7 us
    all_gather x1, blocking collectives, per_device(): lax.all_gather(values_local, 'ctx', axis=0, tiled=True)  19.8 us
    dot_general x9, matrix products, dot_right_t(): lax.dot_general(left, right, (((1,), (1,)), ((), ())), preferred_element_...  18.7 us
    reshape x1, local copies, waits for them, and re-layouts, per_device(): (dot_left_t(windows, grad_rows) * factor).reshape(channels, kernel, chann...  14.8 us
  transfers between devices with their start and end apart: 7, of which 3 were waited for; matrix products, arithmetic and copies ran while one was open for 14% of the time, Pallas kernels for 0%

commit v1 on v0

v1 whole, which is shorter than its diff:
```python
import functools

import jax
import jax.numpy as jnp
from jax import lax
from jax.experimental import pallas as pl
from jax.experimental.pallas import tpu as pltpu
from jax.sharding import PartitionSpec as P

HEADS = 6
DH = 128
C = 768
KW = 5
POOL = 16
ROWS = 512
TOK = 32
SEG_TOK = 512
CTX = 16
NZ = 8
PLANE = 32
BLK = 48
HALF = 384
XW = 256
EPSILON = 1e-06
GELU_SCALE = 0.7978845608028654
CUBIC = 0.044715
MESH = pl.DeviceIdType.MESH
F32 = jnp.float32
BF16 = jnp.bfloat16


def dot(a, b):
    return jnp.dot(a, b, preferred_element_type=F32)


def dot_rt(a, b):
    return lax.dot_general(a, b, (((1,), (1,)), ((), ())), preferred_element_type=F32)


def window_matrix(first, columns):
    row = lax.broadcasted_iota(jnp.int32, (KW * TOK, columns), 0)
    low = (row % TOK) * POOL + row // TOK - 2
    place = lax.broadcasted_iota(jnp.int32, (KW * TOK, columns), 1) + first
    return jnp.where((place >= low) & (place < low + POOL), 1.0, 0.0).astype(BF16)


def body(
    feat_h, base_h, table_h, gain_h, wc_h, wq_h, wk_h, wv_h, wo_h, cot_h,
    grad_in_ref, grad_conv_ref,
    feat, base, table, gain, wc, wq, wk, wv, wo, cot,
    emb, act, normed, inv, slope, win, halo, xs, xr, xt,
    qs, hb, pt, gst, go, gb, grp, grr, grh, grs, rs, rr, edge,
    in_sem, send_sem, recv_sem,
):
    dp = lax.axis_index("dp")
    ctx = lax.axis_index("ctx")
    zz = dp // 2
    hi = dp % 2
    me = hi * CTX + ctx

    def plane_id(p):
        return {"dp": zz * 2 + p // CTX, "ctx": p % CTX}

    def z_id(z):
        return {"dp": z * 2 + hi, "ctx": ctx}

    pairs = [
        (base_h, base), (table_h, table), (gain_h, gain), (feat_h, feat), (cot_h, cot), (wo_h, wo),
        (wc_h, wc), (wq_h, wq), (wk_h, wk), (wv_h, wv),
    ]
    loads = [pltpu.make_async_copy(s, d, in_sem.at[i]) for i, (s, d) in enumerate(pairs)]
    for load in loads:
        load.start()

    barrier = pltpu.get_barrier_semaphore()

    @pl.loop(1, PLANE)
    def _(i):
        pl.semaphore_signal(barrier, inc=1, device_id=plane_id((me + i) % PLANE), device_id_type=MESH)

    @pl.loop(1, NZ)
    def _(i):
        pl.semaphore_signal(barrier, inc=1, device_id=z_id((zz + i) % NZ), device_id_type=MESH)

    win[...] = window_matrix(0, ROWS)
    for load in loads[:4]:
        load.wait()

    base_col = jnp.broadcast_to(base[...], (128, ROWS)).T
    onehot = jnp.where(
        base_col == lax.broadcasted_iota(jnp.int32, (ROWS, 128), 1), 1.0, 0.0
    ).astype(BF16)
    row_id = lax.broadcasted_iota(jnp.int32, (128, C), 0)
    tab = jnp.zeros((128, C), F32)
    for b in range(4):
        tab = jnp.where(row_id == b, table[b : b + 1, :].astype(F32), tab)
    tab = tab.astype(BF16)
    emb[...] = dot(onehot, tab).astype(BF16)
    gain_f = gain[...].astype(F32)

    def rows_forward(r0):
        rows = pl.ds(r0, POOL)
        s = feat[rows, :].astype(F32) + emb[rows, :].astype(F32)
        scale = lax.rsqrt(jnp.mean(s * s, axis=-1, keepdims=True) + EPSILON)
        n = s * scale
        u = n * gain_f
        t = jnp.tanh(GELU_SCALE * (u + CUBIC * (u * u * u)))
        act[rows, :] = (0.5 * u * (1.0 + t)).astype(BF16)
        normed[rows, :] = n
        inv[rows, :] = scale

    rows_forward(0)
    rows_forward(ROWS - POOL)
    pl.semaphore_wait(barrier, PLANE - 1 + NZ - 1)

    def sides(first, last, into, sem):
        low = pltpu.make_async_remote_copy(
            src_ref=first, dst_ref=into.at[1], send_sem=send_sem.at[sem], recv_sem=recv_sem.at[sem],
            device_id={"dp": dp, "ctx": jnp.maximum(ctx - 1, 0)}, device_id_type=MESH,
        )
        high = pltpu.make_async_remote_copy(
            src_ref=last, dst_ref=into.at[0], send_sem=send_sem.at[sem + 1], recv_sem=recv_sem.at[sem + 1],
            device_id={"dp": dp, "ctx": jnp.minimum(ctx + 1, CTX - 1)}, device_id_type=MESH,
        )

        @pl.when(ctx > 0)
        def _():
            low.start()

        @pl.when(ctx < CTX - 1)
        def _():
            high.start()

        @pl.when(ctx == 0)
        def _():
            into[0] = jnp.zeros((16, C), BF16)

        @pl.when(ctx == CTX - 1)
        def _():
            into[1] = jnp.zeros((16, C), BF16)

        return low, high

    def sides_arrive(copies):
        low, high = copies

        @pl.when(ctx < CTX - 1)
        def _():
            low.wait_recv()

        @pl.when(ctx > 0)
        def _():
            high.wait_recv()

    def sides_sent(copies):
        low, high = copies

        @pl.when(ctx > 0)
        def _():
            low.wait_send()

        @pl.when(ctx < CTX - 1)
        def _():
            high.wait_send()

    act_sides = sides(act.at[pl.ds(0, 16), :], act.at[pl.ds(ROWS - 16, 16), :], halo, 0)

    @pl.loop(1, ROWS // POOL - 1)
    def _(i):
        rows_forward(pl.multiple_of(i * POOL, POOL))

    sums = dot(win[...], act[...])
    mean_rows = win[2 * TOK : 3 * TOK, :]
    counts = dot(mean_rows, onehot).astype(BF16)
    pooled_in = dot(mean_rows, feat[...]) + dot(counts, tab)

    loads[4].wait()
    loads[5].wait()
    grad_attn = dot_rt(cot[...], wo[...]).astype(BF16)
    for h in range(HEADS):
        qs[h, 3] = grad_attn[:, h * DH : (h + 1) * DH]

    sides_arrive(act_sides)
    edge_win = jnp.concatenate([window_matrix(-16, 16), window_matrix(ROWS, 16)], axis=1)
    sums = sums + dot(edge_win, jnp.concatenate([halo[0], halo[1]], axis=0))
    high_part = sums.astype(BF16)
    low_part = (sums - high_part.astype(F32)).astype(BF16)

    loads[6].wait()
    conv = jnp.zeros((2 * TOK, C), F32)
    for j in range(KW):
        part = slice(j * TOK, (j + 1) * TOK)
        conv = conv + dot(jnp.concatenate([high_part[part], low_part[part]], axis=0), wc[j])
    pooled = ((pooled_in + conv[:TOK] + conv[TOK:]) * (1.0 / POOL)).astype(BF16)

    for i in range(7, 10):
        loads[i].wait()
    for k, weight in enumerate((wq, wk, wv)):
        made = dot(pooled, weight[...]).astype(BF16)
        for h in range(HEADS):
            qs[h, k] = made[:, h * DH : (h + 1) * DH]

    def to_head(h):
        return pltpu.make_async_remote_copy(
            src_ref=qs.at[h], dst_ref=hb.at[:, pl.ds(pl.multiple_of(ctx * TOK, TOK), TOK), :],
            send_sem=send_sem.at[4 + h], recv_sem=recv_sem.at[4],
            device_id={"dp": dp, "ctx": 2 * h}, device_id_type=MESH,
        )

    for h in range(HEADS):
        @pl.when(ctx != 2 * h)
        def _():
            to_head(h).start()

    for c in range(CTX):
        cols = [sums[j * TOK : (j + 1) * TOK, c * BLK : (c + 1) * BLK] for j in range(KW)]
        cols.append(jnp.zeros((TOK, XW - KW * BLK), F32))
        xs[c] = jnp.concatenate(cols, axis=1).astype(BF16)

    @pl.loop(1, PLANE)
    def _(i):
        p = (me + i) % PLANE
        pltpu.make_async_remote_copy(
            src_ref=xs.at[p % CTX], dst_ref=xr.at[me], send_sem=send_sem.at[10], recv_sem=recv_sem.at[5],
            device_id=plane_id(p), device_id_type=MESH,
        ).start()

    xr[me] = xs[ctx]

    head = ctx // 2
    is_head = (ctx % 2 == 0) & (ctx < 2 * HEADS)

    def from_head(c):
        return pltpu.make_async_remote_copy(
            src_ref=go.at[:, pl.ds(pl.multiple_of(c * TOK, TOK), TOK), :], dst_ref=gb.at[head],
            send_sem=send_sem.at[11], recv_sem=recv_sem.at[6],
            device_id={"dp": dp, "ctx": c}, device_id_type=MESH,
        )

    @pl.when(is_head)
    def _():
        hb[:, pl.ds(pl.multiple_of(ctx * TOK, TOK), TOK), :] = qs[head]
        arrived = hb.at[:, pl.ds(0, SEG_TOK - TOK), :]
        pltpu.make_async_copy(arrived, arrived, recv_sem.at[4]).wait()
        scale = 1.0 / DH**0.5
        keys = hb[1]
        values = hb[2]
        values_t = values.T

        @pl.loop(0, SEG_TOK // 128)
        def _(i):
            part = pl.ds(pl.multiple_of(i * 128, 128), 128)
            query = hb[0, part, :]
            grad = hb[3, part, :]
            score = dot_rt(keys, query) * scale
            expo = jnp.exp(score - jnp.max(score, axis=0, keepdims=True))
            prob = expo * (1.0 / jnp.sum(expo, axis=0, keepdims=True))
            prob_b = prob.astype(BF16)
            out_t = dot(values_t, prob_b).astype(BF16).astype(F32)
            delta = jnp.sum(grad.T.astype(F32) * out_t, axis=0, keepdims=True)
            grad_prob = dot_rt(values, grad)
            pt[:, part] = prob_b
            gst[:, part] = (prob * (grad_prob - delta) * scale).astype(BF16)

        go[0] = dot(keys.T, gst[...]).T.astype(BF16)
        go[1] = dot(gst[...], hb[0]).astype(BF16)
        go[2] = dot(pt[...], hb[3]).astype(BF16)

        @pl.loop(1, CTX)
        def _(i):
            from_head((ctx + i) % CTX).start()

        gb[head] = go[:, pl.ds(pl.multiple_of(ctx * TOK, TOK), TOK), :]
        five = gb.at[pl.ds(0, HEADS - 1)]
        pltpu.make_async_copy(five, five, recv_sem.at[6]).wait()

    @pl.when(jnp.logical_not(is_head))
    def _():
        pltpu.make_async_copy(gb, gb, recv_sem.at[6]).wait()

    grad_pooled = cot[...].astype(F32)
    for k, weight in enumerate((wq, wk, wv)):
        whole = jnp.concatenate([gb[h, k] for h in range(HEADS)], axis=1)
        grad_pooled = grad_pooled + dot_rt(whole, weight[...])
    grad_f = (grad_pooled * (1.0 / POOL)).astype(BF16).astype(F32)
    grs[...] = grad_f.astype(BF16)
    for h in range(2):
        cols = [grad_f[:, (2 * z + h) * BLK : (2 * z + h + 1) * BLK] for z in range(NZ)]
        grp[h] = jnp.concatenate(cols, axis=1).astype(BF16)

    @pl.loop(1, PLANE)
    def _(i):
        p = (me + i) % PLANE
        pltpu.make_async_remote_copy(
            src_ref=grp.at[p // CTX], dst_ref=grr.at[me], send_sem=send_sem.at[12], recv_sem=recv_sem.at[7],
            device_id=plane_id(p), device_id_type=MESH,
        ).start()

    grr[me] = grp[hi]
    row_sides = sides(grs.at[pl.ds(0, 16), :], grs.at[pl.ds(16, 16), :], grh, 2)

    @pl.loop(0, ROWS // POOL)
    def _(i):
        rows = pl.ds(pl.multiple_of(i * POOL, POOL), POOL)
        u = normed[rows, :] * gain_f
        square = u * u
        t = jnp.tanh(GELU_SCALE * (u + CUBIC * (square * u)))
        d = 0.5 * (1.0 + t) + 0.5 * u * (1.0 - t * t) * GELU_SCALE * (1.0 + 3.0 * CUBIC * square)
        slope[rows, :] = d * gain_f

    others = xr.at[pl.ds(0, PLANE - 1)]
    pltpu.make_async_copy(others, others, recv_sem.at[5]).wait()
    for i in range(PLANE * TOK // 128):
        block = jnp.concatenate([xr[4 * i + k] for k in range(4)], axis=0)
        xt[:, i * 128 : (i + 1) * 128] = block.T

    others = grr.at[pl.ds(0, PLANE - 1)]
    pltpu.make_async_copy(others, others, recv_sem.at[7]).wait()
    factor = 1.0 / (CTX * CTX * ROWS) ** 0.5
    made = dot(xt[...], grr[...].reshape(PLANE * TOK, HALF)) * factor
    rs[...] = made.T.astype(BF16)

    @pl.loop(1, NZ)
    def _(i):
        z = (zz + i) % NZ
        pltpu.make_async_remote_copy(
            src_ref=rs.at[pl.ds(pl.multiple_of(z * BLK, 16), BLK), :], dst_ref=rr.at[zz],
            send_sem=send_sem.at[13], recv_sem=recv_sem.at[8],
            device_id=z_id(z), device_id_type=MESH,
        ).start()

    rr[zz] = rs[pl.ds(pl.multiple_of(zz * BLK, 16), BLK), :]

    sides_arrive(row_sides)
    ext = jnp.concatenate([grh[0], grs[...], grh[1]], axis=0)
    first0 = first1 = mid = last0 = last1 = None
    for j in range(KW):
        y = dot_rt(ext, wc[j])
        own, before, after = y[16:48], y[15:47], y[17:49]
        terms = (
            before if j >= 3 else own,
            before if j >= 4 else own,
            own,
            after if j < 1 else own,
            after if j < 2 else own,
        )
        if j == 0:
            first0, first1, mid, last0, last1 = terms
        else:
            first0, first1, mid, last0, last1 = (
                a + b for a, b in zip((first0, first1, mid, last0, last1), terms)
            )
    for k, value in enumerate((first0, first1, mid, last0, last1, grs[...].astype(F32))):
        edge[k] = value

    in_group = lax.broadcasted_iota(jnp.int32, (POOL, C), 0)

    @pl.loop(0, TOK)
    def _(i):
        rows = pl.ds(pl.multiple_of(i * POOL, POOL), POOL)
        one = pl.ds(i, 1)
        g = jnp.broadcast_to(edge[2, one, :], (POOL, C))
        for r, k in ((0, 0), (1, 1), (14, 3), (15, 4)):
            g = jnp.where(in_group == r, edge[k, one, :], g)
        g = g * slope[rows, :]
        n = normed[rows, :]
        mean = jnp.mean(g * n, axis=-1, keepdims=True)
        grad_in_ref[rows, :] = (edge[5, one, :] + inv[rows, :] * (g - n * mean)).astype(BF16)

    others = rr.at[pl.ds(0, NZ - 1)]
    pltpu.make_async_copy(others, others, recv_sem.at[8]).wait()
    total = rr[0].astype(F32)
    for z in range(1, NZ):
        total = total + rr[z].astype(F32)
    grad_conv_ref[...] = total

    sides_sent(act_sides)
    sides_sent(row_sides)
    for h in range(HEADS):
        @pl.when(ctx != 2 * h)
        def _():
            to_head(h).wait_send()
    part = xr.at[pl.ds(0, PLANE - 1)]
    pltpu.make_async_copy(part, part, send_sem.at[10]).wait()

    @pl.when(is_head)
    def _():
        part = go.at[:, pl.ds(0, SEG_TOK - TOK), :]
        pltpu.make_async_copy(part, part, send_sem.at[11]).wait()

    part = grr.at[pl.ds(0, PLANE - 1)]
    pltpu.make_async_copy(part, part, send_sem.at[12]).wait()
    part = rr.at[pl.ds(0, NZ - 1)]
    pltpu.make_async_copy(part, part, send_sem.at[13]).wait()


def per_device(
    features, bases, dna_table, norm_gain, w_conv, w_query, w_key, w_value, w_out, cotangent
):
    vmem = pltpu.VMEM
    scratch = [
        vmem((ROWS, C), BF16), vmem((1, ROWS), jnp.int32), vmem((4, C), BF16), vmem((1, C), BF16),
        vmem((KW, C, C), BF16), vmem((C, C), BF16), vmem((C, C), BF16), vmem((C, C), BF16),
        vmem((C, C), BF16), vmem((TOK, C), BF16),
        vmem((ROWS, C), BF16),
        vmem((ROWS, C), BF16),
        vmem((ROWS, C), F32),
        vmem((ROWS, 1), F32),
        vmem((ROWS, C), F32),
        vmem((KW * TOK, ROWS), BF16),
        vmem((2, 16, C), BF16),
        vmem((CTX, TOK, XW), BF16),
        vmem((PLANE, TOK, XW), BF16),
        vmem((XW, PLANE * TOK), BF16),
        vmem((HEADS, 4, TOK, DH), BF16),
        vmem((4, SEG_TOK, DH), BF16),
        vmem((SEG_TOK, SEG_TOK), BF16),
        vmem((SEG_TOK, SEG_TOK), BF16),
        vmem((3, SEG_TOK, DH), BF16),
        vmem((HEADS, 3, TOK, DH), BF16),
        vmem((2, TOK, HALF), BF16),
        vmem((PLANE, TOK, HALF), BF16),
        vmem((2, 16, C), BF16),
        vmem((TOK, C), BF16),
        vmem((HALF, XW), BF16),
        vmem((NZ, BLK, XW), BF16),
        vmem((6, TOK, C), F32),
        pltpu.SemaphoreType.DMA((10,)),
        pltpu.SemaphoreType.DMA((14,)),
        pltpu.SemaphoreType.DMA((9,)),
    ]
    grad_in, grad_conv = pl.pallas_call(
        body,
        out_shape=(
            jax.ShapeDtypeStruct((ROWS, C), BF16),
            jax.ShapeDtypeStruct((BLK, XW), F32),
        ),
        in_specs=[pl.BlockSpec(memory_space=pl.ANY)] * 10,
        out_specs=(pl.BlockSpec(memory_space=pltpu.VMEM),) * 2,
        scratch_shapes=scratch,
        compiler_params=pltpu.CompilerParams(
            collective_id=0, has_side_effects=True, vmem_limit_bytes=48 * 1024 * 1024
        ),
        cost_estimate=pl.CostEstimate(flops=10**9, bytes_accessed=12 * 10**6, transcendentals=10**6),
    )(
        features[0], bases, dna_table, norm_gain[None], w_conv, w_query, w_key, w_value, w_out,
        cotangent[0],
    )
    grad_conv = grad_conv[:, : KW * BLK].reshape(BLK, KW, BLK).transpose(2, 1, 0)
    return grad_in[None], grad_conv


def solution(mesh):
    in_specs = (
        P("dp", "ctx", None),
        P("dp", "ctx"),
        P(),
        P(),
        P(),
        P(),
        P(),
        P(),
        P(),
        P("dp", "ctx", None),
    )
    out_specs = (P("dp", "ctx", None), P("ctx", None, "dp"))
    return jax.shard_map(
        per_device, mesh=mesh, in_specs=in_specs, out_specs=out_specs, check_vma=False
    )
```

time: 536 us -> 68.4 us (0.13); the launches traced: 529 us -> 68 us
  waiting for transfers between devices: 325 us -> 0 us
  local copies, waits for them, and re-layouts: 71.8 us -> 9.43 us
  Pallas kernels: 0 us -> 57.9 us
  matrix products: 48.2 us -> 0 us
  blocking collectives: 43.5 us -> 0 us
  starting transfers between devices: 15.5 us -> 0 us
  between operations: 14.1 us -> 0.65 us
  other arithmetic: 11.5 us -> 0 us
    unnamed x5 -> x0, waiting for transfers between devices: 227 us -> none
    reduce_scatter x1 -> x0, waiting for transfers between devices: 97.3 us -> none  [per_device(): lax.psum_scatter(whole_terms, 'ctx', scatter_dimension=0, tiled=True)]
    pallas_call x0 -> x1, Pallas kernels: none -> 57.9 us  [per_device(): pl.pallas_call(body, out_shape=(jax.ShapeDtypeStruct((ROWS, C), BF16), ja...]
    dot_general x25 -> x0, matrix products: 48.2 us -> none  [the longest x9 18.7 us: dot_right_t(): lax.dot_general(left, right, (((1,), (1,)), ((), ())), preferred_element_...]
    all_gather x2 -> x0, blocking collectives: 43.5 us -> none  [the longest x1 23.7 us: per_device(): lax.all_gather(keys_local, 'ctx', axis=0, tiled=True)]
    unnamed x42 -> x15, local copies, waits for them, and re-layouts: 35.3 us -> 7.99 us
    reshape x2 -> x0, local copies, waits for them, and re-layouts: 23.4 us -> none  [the longest x1 14.8 us: per_device(): (dot_left_t(windows, grad_rows) * factor).reshape(channels, kernel, chann...]
    ppermute x4 -> x0, starting transfers between devices: 15.2 us -> none  [the longest x2 8.44 us: extended(): lax.ppermute(lax.slice_in_dim(block, 0, width, axis=dim), axis, backward)]
  transfers between devices with their start and end apart: 7 -> 0, of which waited for: 3 -> 0; matrix products, arithmetic and copies ran while one was open for 14% -> 0% of each run, Pallas kernels for 0% -> 0%
where the time goes in v1:
time: 68.4 us; the launch traced here: 68 us
  Pallas kernels  57.9 us (85%)
  local copies, waits for them, and re-layouts  9.43 us (14%)
    pallas_call x1, Pallas kernels, per_device(): pl.pallas_call(body, out_shape=(jax.ShapeDtypeStruct((ROWS, C), BF16), ja...  57.9 us
    unnamed x15, local copies, waits for them, and re-layouts  7.99 us

profile of v1, /device:TPU:1, one launch (start us, length us, event | category | flops | bytes accessed | tf_op | source)
XLA Modules:
  0.0 68.0 jit_solution(10029519317672364513)
XLA Ops:
  0.6 0.7 %broadcast_in_dim.6.gain_h = bf16[1,768]{1,0:T(2,128)(2,1)S(1)} reshape(bf16[768]{0:T(1024)(128)(2,1)} %param.13) | data formatting | bytes 3072 | tf_op jit(solution)/shard_map/broadcast_in_dim | solution.py:446
  1.3 0.0 copy-start
  1.3 1.3 %copy-done = bf16[768,768]{1,0:T(8,128)(2,1)S(1)} copy-done((bf16[768,768]{1,0:T(8,128)(2,1)S(1)}, bf16[768,768]{1,0:T(8,128)(2,1)}, u32[]{:S(2)}) %copy-start) | copy-done | bytes 1179672
  2.6 0.0 copy-start.1
  2.6 1.3 %copy-done.1 = bf16[768,768]{1,0:T(8,128)(2,1)S(1)} copy-done((bf16[768,768]{1,0:T(8,128)(2,1)S(1)}, bf16[768,768]{1,0:T(8,128)(2,1)}, u32[]{:S(2)}) %copy-start.1) | copy-done | bytes 1179672
  3.9 0.0 copy-start.2
  3.9 1.3 %copy-done.2 = bf16[768,768]{1,0:T(8,128)(2,1)S(1)} copy-done((bf16[768,768]{1,0:T(8,128)(2,1)S(1)}, bf16[768,768]{1,0:T(8,128)(2,1)}, u32[]{:S(2)}) %copy-start.2) | copy-done | bytes 1179672
  5.1 0.0 copy-start.3
  5.1 1.1 %copy-done.3 = bf16[1,512,768]{2,1,0:T(8,128)(2,1)S(1)} copy-done((bf16[1,512,768]{2,1,0:T(8,128)(2,1)S(1)}, bf16[1,512,768]{2,1,0:T(8,128)(2,1)}, u32[]{:S(2)}) %copy-start.3) | copy-done | bytes 786456
  6.3 0.0 copy-start.4
  6.3 0.8 %copy-done.4 = bf16[1,32,768]{2,1,0:T(8,128)(2,1)S(1)} copy-done((bf16[1,32,768]{2,1,0:T(8,128)(2,1)S(1)}, bf16[1,32,768]{2,1,0:T(8,128)(2,1)}, u32[]{:S(2)}) %copy-start.4) | copy-done | bytes 49176
  7.1 0.0 copy-start.5
  7.1 0.7 %copy-done.5 = bf16[4,768]{1,0:T(4,128)(2,1)S(1)} copy-done((bf16[4,768]{1,0:T(4,128)(2,1)S(1)}, bf16[4,768]{1,0:T(4,128)(2,1)}, u32[]{:S(2)}) %copy-start.5) | copy-done | bytes 6168
  7.8 0.0 copy-start.6
  7.8 0.7 copy-done.6
  8.4 57.9 %shard_map.113 = (bf16[512,768]{1,0:T(8,128)(2,1)S(1)}, f32[48,256]{1,0:T(8,128)S(1)}) custom-call(bf16[512,768]{1,0:T(8,128)(2,1)S(1)} %bitcast.7, s32[1,512]{1,0:T(1,128)S(1)} %copy-done.6, bf16[4,768]{1,0:T(4,128)(2,1)S(1)} %copy-done.5, bf16[1,768]{1,0:T(2,128)(2,1)S(1)} %broadcast_in_dim.6.gain_h, bf16[5,768,768]{2,1,0:T(8,128)(2,1)} %wc_h.1, ...), custom_call_target="tpu_custom_call" | custom-call | flops 1000000000 | bytes 12000000 | tf_op jit(solution)/shard_map/pallas_call | solution.py:432
  66.4 0.7 %copy.13 = f32[48,240]{0,1:T(8,128)} copy(f32[48,240]{1,0:T(8,128)S(1)} %bitcast.10) | data formatting | bytes 92160 | tf_op jit(solution)/shard_map/slice | solution.py:449
  67.1 0.9 %copy.15 = bf16[1,512,768]{2,1,0:T(8,128)(2,1)} copy(bf16[1,512,768]{2,1,0:T(8,128)(2,1)S(1)} %bitcast.8) | data formatting | bytes 1572864
Async XLA Ops:
  1.3 1.3 %copy-start = (bf16[768,768]{1,0:T(8,128)(2,1)S(1)}, bf16[768,768]{1,0:T(8,128)(2,1)}, u32[]{:S(2)}) copy-start(bf16[768,768]{1,0:T(8,128)(2,1)} %wq_h.1) | copy-start | bytes 3538948
  2.6 1.3 %copy-start.1 = (bf16[768,768]{1,0:T(8,128)(2,1)S(1)}, bf16[768,768]{1,0:T(8,128)(2,1)}, u32[]{:S(2)}) copy-start(bf16[768,768]{1,0:T(8,128)(2,1)} %wk_h.1) | copy-start | bytes 3538948
  3.9 1.3 %copy-start.2 = (bf16[768,768]{1,0:T(8,128)(2,1)S(1)}, bf16[768,768]{1,0:T(8,128)(2,1)}, u32[]{:S(2)}) copy-start(bf16[768,768]{1,0:T(8,128)(2,1)} %wv_h.1) | copy-start | bytes 3538948
  5.1 1.1 %copy-start.3 = (bf16[1,512,768]{2,1,0:T(8,128)(2,1)S(1)}, bf16[1,512,768]{2,1,0:T(8,128)(2,1)}, u32[]{:S(2)}) copy-start(bf16[1,512,768]{2,1,0:T(8,128)(2,1)} %param.10) | copy-start | bytes 2359300
  6.3 0.8 %copy-start.4 = (bf16[1,32,768]{2,1,0:T(8,128)(2,1)S(1)}, bf16[1,32,768]{2,1,0:T(8,128)(2,1)}, u32[]{:S(2)}) copy-start(bf16[1,32,768]{2,1,0:T(8,128)(2,1)} %param.19) | copy-start | bytes 147460
  7.1 0.7 %copy-start.5 = (bf16[4,768]{1,0:T(4,128)(2,1)S(1)}, bf16[4,768]{1,0:T(4,128)(2,1)}, u32[]{:S(2)}) copy-start(bf16[4,768]{1,0:T(4,128)(2,1)} %table_h.1) | copy-start | bytes 18436
  7.8 0.7 %copy-start.6 = (s32[1,512]{1,0:T(1,128)S(1)}, s32[1,512]{1,0:T(1,128)}, u32[]{:S(2)}) copy-start(s32[1,512]{1,0:T(1,128)} %base_h.1) | copy-start | bytes 6148

commit v2 on v1

--- a/solution.py
+++ b/solution.py
@@ -19,7 +19,9 @@
 NZ = 8
 PLANE = 32
 BLK = 48
-HALF = 384
+PARTS = 3
+SUB = 16
+CHIPS = 16
 XW = 256
 EPSILON = 1e-06
 GELU_SCALE = 0.7978845608028654
@@ -49,7 +51,7 @@
     grad_in_ref, grad_conv_ref,
     feat, base, table, gain, wc, wq, wk, wv, wo, cot,
     emb, act, normed, inv, slope, win, halo, xs, xr, xt,
-    qs, hb, pt, gst, go, gb, grp, grr, grh, grs, rs, rr, edge,
+    qs, hb, pt, gst, go, gb, perm, grp, grr, grh, grs, rs, rr, edge,
     in_sem, send_sem, recv_sem,
 ):
     dp = lax.axis_index("dp")
@@ -57,6 +59,9 @@
     zz = dp // 2
     hi = dp % 2
     me = hi * CTX + ctx
+    core = ctx % 2
+    chip = me // 2
+    slot = core * CHIPS + chip
 
     def plane_id(p):
         return {"dp": zz * 2 + p // CTX, "ctx": p % CTX}
@@ -83,6 +88,10 @@
         pl.semaphore_signal(barrier, inc=1, device_id=z_id((zz + i) % NZ), device_id_type=MESH)
 
     win[...] = window_matrix(0, ROWS)
+    col = lax.broadcasted_iota(jnp.int32, (C, C), 1)
+    group = col // 128
+    channel = (2 * (col % 128 // SUB) + group % 2) * BLK + group // 2 * SUB + col % SUB
+    perm[...] = jnp.where(channel == lax.broadcasted_iota(jnp.int32, (C, C), 0), 1.0, 0.0).astype(BF16)
     for load in loads[:4]:
         load.wait()
 
@@ -96,7 +105,7 @@
         tab = jnp.where(row_id == b, table[b : b + 1, :].astype(F32), tab)
     tab = tab.astype(BF16)
     emb[...] = dot(onehot, tab).astype(BF16)
-    gain_f = gain[...].astype(F32)
+    gain_f = gain[...].astype(F32)[None]
 
     def rows_forward(r0):
         rows = pl.ds(r0, POOL)
@@ -111,6 +120,10 @@
 
     rows_forward(0)
     rows_forward(ROWS - POOL)
+    @pl.loop(1, ROWS // POOL // 2)
+    def _(i):
+        rows_forward(pl.multiple_of(i * POOL, POOL))
+
     pl.semaphore_wait(barrier, PLANE - 1 + NZ - 1)
 
     def sides(first, last, into, sem):
@@ -165,7 +178,7 @@
 
     act_sides = sides(act.at[pl.ds(0, 16), :], act.at[pl.ds(ROWS - 16, 16), :], halo, 0)
 
-    @pl.loop(1, ROWS // POOL - 1)
+    @pl.loop(ROWS // POOL // 2, ROWS // POOL - 1)
     def _(i):
         rows_forward(pl.multiple_of(i * POOL, POOL))
 
@@ -185,6 +198,23 @@
     sums = sums + dot(edge_win, jnp.concatenate([halo[0], halo[1]], axis=0))
     high_part = sums.astype(BF16)
     low_part = (sums - high_part.astype(F32)).astype(BF16)
+
+    for c in range(CTX):
+        cols = [sums[j * TOK : (j + 1) * TOK, c * BLK : (c + 1) * BLK] for j in range(KW)]
+        cols.append(jnp.zeros((TOK, XW - KW * BLK), F32))
+        xs[c] = jnp.concatenate(cols, axis=1).astype(BF16)
+
+    other = 1 - hi
+
+    def x_send(half, c):
+        return pltpu.make_async_remote_copy(
+            src_ref=xs.at[c], dst_ref=xr.at[slot], send_sem=send_sem.at[10], recv_sem=recv_sem.at[5],
+            device_id={"dp": zz * 2 + half, "ctx": c}, device_id_type=MESH,
+        )
+
+    @pl.loop(1, CTX)
+    def _(i):
+        x_send(hi, (ctx + i) % CTX).start()
 
     loads[6].wait()
     conv = jnp.zeros((2 * TOK, C), F32)
@@ -212,27 +242,18 @@
         def _():
             to_head(h).start()
 
-    for c in range(CTX):
-        cols = [sums[j * TOK : (j + 1) * TOK, c * BLK : (c + 1) * BLK] for j in range(KW)]
-        cols.append(jnp.zeros((TOK, XW - KW * BLK), F32))
-        xs[c] = jnp.concatenate(cols, axis=1).astype(BF16)
-
-    @pl.loop(1, PLANE)
-    def _(i):
-        p = (me + i) % PLANE
-        pltpu.make_async_remote_copy(
-            src_ref=xs.at[p % CTX], dst_ref=xr.at[me], send_sem=send_sem.at[10], recv_sem=recv_sem.at[5],
-            device_id=plane_id(p), device_id_type=MESH,
-        ).start()
-
-    xr[me] = xs[ctx]
+    @pl.loop(0, CTX)
+    def _(i):
+        x_send(other, (ctx + i) % CTX).start()
+
+    xr[slot] = xs[ctx]
 
     head = ctx // 2
     is_head = (ctx % 2 == 0) & (ctx < 2 * HEADS)
 
     def from_head(c):
         return pltpu.make_async_remote_copy(
-            src_ref=go.at[:, pl.ds(pl.multiple_of(c * TOK, TOK), TOK), :], dst_ref=gb.at[head],
+            src_ref=go.at[c], dst_ref=gb.at[head],
             send_sem=send_sem.at[11], recv_sem=recv_sem.at[6],
             device_id={"dp": dp, "ctx": c}, device_id_type=MESH,
         )
@@ -262,15 +283,15 @@
             pt[:, part] = prob_b
             gst[:, part] = (prob * (grad_prob - delta) * scale).astype(BF16)
 
-        go[0] = dot(keys.T, gst[...]).T.astype(BF16)
-        go[1] = dot(gst[...], hb[0]).astype(BF16)
-        go[2] = dot(pt[...], hb[3]).astype(BF16)
+        go[:, 0] = dot(keys.T, gst[...]).T.astype(BF16).reshape(CTX, TOK, DH)
+        go[:, 1] = dot(gst[...], hb[0]).astype(BF16).reshape(CTX, TOK, DH)
+        go[:, 2] = dot(pt[...], hb[3]).astype(BF16).reshape(CTX, TOK, DH)
 
         @pl.loop(1, CTX)
         def _(i):
             from_head((ctx + i) % CTX).start()
 
-        gb[head] = go[:, pl.ds(pl.multiple_of(ctx * TOK, TOK), TOK), :]
+        gb[head] = go[ctx]
         five = gb.at[pl.ds(0, HEADS - 1)]
         pltpu.make_async_copy(five, five, recv_sem.at[6]).wait()
 
@@ -282,21 +303,25 @@
     for k, weight in enumerate((wq, wk, wv)):
         whole = jnp.concatenate([gb[h, k] for h in range(HEADS)], axis=1)
         grad_pooled = grad_pooled + dot_rt(whole, weight[...])
-    grad_f = (grad_pooled * (1.0 / POOL)).astype(BF16).astype(F32)
-    grs[...] = grad_f.astype(BF16)
-    for h in range(2):
-        cols = [grad_f[:, (2 * z + h) * BLK : (2 * z + h + 1) * BLK] for z in range(NZ)]
-        grp[h] = jnp.concatenate(cols, axis=1).astype(BF16)
-
-    @pl.loop(1, PLANE)
-    def _(i):
-        p = (me + i) % PLANE
-        pltpu.make_async_remote_copy(
-            src_ref=grp.at[p // CTX], dst_ref=grr.at[me], send_sem=send_sem.at[12], recv_sem=recv_sem.at[7],
-            device_id=plane_id(p), device_id_type=MESH,
-        ).start()
-
-    grr[me] = grp[hi]
+    grs[...] = (grad_pooled * (1.0 / POOL)).astype(BF16)
+    sorted_g = dot(grs[...], perm[...]).astype(BF16)
+    for k in range(PARTS):
+        for h in range(2):
+            first = (2 * k + h) * 128
+            grp[k, h] = sorted_g[:, first : first + 128]
+
+    for k in range(PARTS):
+        @pl.loop(1, CHIPS)
+        def _(i):
+            to = (chip + i) % CHIPS
+            pltpu.make_async_remote_copy(
+                src_ref=grp.at[k, to // (CHIPS // 2)], dst_ref=grr.at[k, slot],
+                send_sem=send_sem.at[12], recv_sem=recv_sem.at[7 + k],
+                device_id=plane_id(2 * to + core), device_id_type=MESH,
+            ).start()
+
+        grr[k, slot] = grp[k, hi]
+
     row_sides = sides(grs.at[pl.ds(0, 16), :], grs.at[pl.ds(16, 16), :], grh, 2)
 
     @pl.loop(0, ROWS // POOL)
@@ -311,25 +336,45 @@
     others = xr.at[pl.ds(0, PLANE - 1)]
     pltpu.make_async_copy(others, others, recv_sem.at[5]).wait()
     for i in range(PLANE * TOK // 128):
-        block = jnp.concatenate([xr[4 * i + k] for k in range(4)], axis=0)
+        block = xr[4 * i : 4 * i + 4].reshape(128, XW)
         xt[:, i * 128 : (i + 1) * 128] = block.T
 
-    others = grr.at[pl.ds(0, PLANE - 1)]
-    pltpu.make_async_copy(others, others, recv_sem.at[7]).wait()
     factor = 1.0 / (CTX * CTX * ROWS) ** 0.5
-    made = dot(xt[...], grr[...].reshape(PLANE * TOK, HALF)) * factor
-    rs[...] = made.T.astype(BF16)
-
-    @pl.loop(1, NZ)
-    def _(i):
-        z = (zz + i) % NZ
-        pltpu.make_async_remote_copy(
-            src_ref=rs.at[pl.ds(pl.multiple_of(z * BLK, 16), BLK), :], dst_ref=rr.at[zz],
-            send_sem=send_sem.at[13], recv_sem=recv_sem.at[8],
-            device_id=z_id(z), device_id_type=MESH,
-        ).start()
-
-    rr[zz] = rs[pl.ds(pl.multiple_of(zz * BLK, 16), BLK), :]
+
+    def pass_on(k):
+        mine = grr.at[k, pl.ds(pl.multiple_of(core * CHIPS, CHIPS), CHIPS)]
+        return pltpu.make_async_remote_copy(
+            src_ref=mine, dst_ref=mine, send_sem=send_sem.at[14 + k], recv_sem=recv_sem.at[11 + k],
+            device_id={"dp": dp, "ctx": ctx + 1 - 2 * core}, device_id_type=MESH,
+        )
+
+    def forward(k):
+        others = grr.at[k, pl.ds(0, CHIPS - 1)]
+        pltpu.make_async_copy(others, others, recv_sem.at[7 + k]).wait()
+        pass_on(k).start()
+
+    def multiply(k):
+        pass_on(k).wait_recv()
+        made = dot(xt[...], grr[k].reshape(PLANE * TOK, 128)) * factor
+        rs[k] = made.T.astype(BF16)
+
+        @pl.loop(1, NZ)
+        def _(i):
+            z = (zz + i) % NZ
+            pltpu.make_async_remote_copy(
+                src_ref=rs.at[k, pl.ds(pl.multiple_of(z * SUB, SUB), SUB), :], dst_ref=rr.at[zz, k],
+                send_sem=send_sem.at[13], recv_sem=recv_sem.at[10],
+                device_id=z_id(z), device_id_type=MESH,
+            ).start()
+
+        rr[zz, k] = rs[k, pl.ds(pl.multiple_of(zz * SUB, SUB), SUB), :]
+
+    forward(0)
+    forward(1)
+    multiply(0)
+    forward(2)
+    multiply(1)
+    multiply(2)
 
     sides_arrive(row_sides)
     ext = jnp.concatenate([grh[0], grs[...], grh[1]], axis=0)
@@ -368,11 +413,11 @@
         grad_in_ref[rows, :] = (edge[5, one, :] + inv[rows, :] * (g - n * mean)).astype(BF16)
 
     others = rr.at[pl.ds(0, NZ - 1)]
-    pltpu.make_async_copy(others, others, recv_sem.at[8]).wait()
+    pltpu.make_async_copy(others, others, recv_sem.at[10]).wait()
     total = rr[0].astype(F32)
     for z in range(1, NZ):
         total = total + rr[z].astype(F32)
-    grad_conv_ref[...] = total
+    grad_conv_ref[...] = total.reshape(BLK, XW)
 
     sides_sent(act_sides)
     sides_sent(row_sides)
@@ -385,11 +430,13 @@
 
     @pl.when(is_head)
     def _():
-        part = go.at[:, pl.ds(0, SEG_TOK - TOK), :]
+        part = go.at[pl.ds(0, CTX - 1)]
         pltpu.make_async_copy(part, part, send_sem.at[11]).wait()
 
-    part = grr.at[pl.ds(0, PLANE - 1)]
+    part = grr.at[:, pl.ds(0, CHIPS - 1)]
     pltpu.make_async_copy(part, part, send_sem.at[12]).wait()
+    for k in range(PARTS):
+        pass_on(k).wait_send()
     part = rr.at[pl.ds(0, NZ - 1)]
     pltpu.make_async_copy(part, part, send_sem.at[13]).wait()
 
@@ -399,7 +446,7 @@
 ):
     vmem = pltpu.VMEM
     scratch = [
-        vmem((ROWS, C), BF16), vmem((1, ROWS), jnp.int32), vmem((4, C), BF16), vmem((1, C), BF16),
+        vmem((ROWS, C), BF16), vmem((1, ROWS), jnp.int32), vmem((4, C), BF16), vmem((C,), BF16),
         vmem((KW, C, C), BF16), vmem((C, C), BF16), vmem((C, C), BF16), vmem((C, C), BF16),
         vmem((C, C), BF16), vmem((TOK, C), BF16),
         vmem((ROWS, C), BF16),
@@ -416,18 +463,19 @@
         vmem((4, SEG_TOK, DH), BF16),
         vmem((SEG_TOK, SEG_TOK), BF16),
         vmem((SEG_TOK, SEG_TOK), BF16),
-        vmem((3, SEG_TOK, DH), BF16),
+        vmem((CTX, 3, TOK, DH), BF16),
         vmem((HEADS, 3, TOK, DH), BF16),
-        vmem((2, TOK, HALF), BF16),
-        vmem((PLANE, TOK, HALF), BF16),
+        vmem((C, C), BF16),
+        vmem((PARTS, 2, TOK, 128), BF16),
+        vmem((PARTS, PLANE, TOK, 128), BF16),
         vmem((2, 16, C), BF16),
         vmem((TOK, C), BF16),
-        vmem((HALF, XW), BF16),
-        vmem((NZ, BLK, XW), BF16),
+        vmem((PARTS, 128, XW), BF16),
+        vmem((NZ, PARTS, SUB, XW), BF16),
         vmem((6, TOK, C), F32),
         pltpu.SemaphoreType.DMA((10,)),
+        pltpu.SemaphoreType.DMA((17,)),
         pltpu.SemaphoreType.DMA((14,)),
-        pltpu.SemaphoreType.DMA((9,)),
     ]
     grad_in, grad_conv = pl.pallas_call(
         body,
@@ -435,15 +483,15 @@
             jax.ShapeDtypeStruct((ROWS, C), BF16),
             jax.ShapeDtypeStruct((BLK, XW), F32),
         ),
-        in_specs=[pl.BlockSpec(memory_space=pl.ANY)] * 10,
+        in_specs=[pl.BlockSpec(memory_space=pltpu.HBM)] * 10,
         out_specs=(pl.BlockSpec(memory_space=pltpu.VMEM),) * 2,
         scratch_shapes=scratch,
         compiler_params=pltpu.CompilerParams(
-            collective_id=0, has_side_effects=True, vmem_limit_bytes=48 * 1024 * 1024
+            collective_id=0, has_side_effects=True, vmem_limit_bytes=56 * 1024 * 1024
         ),
         cost_estimate=pl.CostEstimate(flops=10**9, bytes_accessed=12 * 10**6, transcendentals=10**6),
     )(
-        features[0], bases, dna_table, norm_gain[None], w_conv, w_query, w_key, w_value, w_out,
+        features[0], bases, dna_table, norm_gain, w_conv, w_query, w_key, w_value, w_out,
         cotangent[0],
     )
     grad_conv = grad_conv[:, : KW * BLK].reshape(BLK, KW, BLK).transpose(2, 1, 0)

time: 68.4 us -> 57.1 us (0.83)
  local copies, waits for them, and re-layouts: 9.43 us -> 3.61 us
  Pallas kernels: 57.9 us -> 52.7 us
    unnamed x15 -> x1, local copies, waits for them, and re-layouts: 7.99 us -> 2.06 us
    pallas_call x1, Pallas kernels: 57.9 us -> 52.7 us  [per_device(): pl.pallas_call(body, out_shape=(jax.ShapeDtypeStruct((ROWS, C), BF16), ja...]
    slice x1, local copies, waits for them, and re-layouts: 0.75 us -> 1.55 us  [per_device(): grad_conv = grad_conv[:, :KW * BLK].reshape(BLK, KW, BLK).transpose(2, 1, 0)]
    broadcast_in_dim x1 -> x0, local copies, waits for them, and re-layouts: 0.69 us -> none  [per_device(): norm_gain[None]]
where the time goes in v2:
time: 57.1 us; the launch traced here: 56.9 us
  Pallas kernels  52.7 us (92%)
  local copies, waits for them, and re-layouts  3.61 us (6%)
  between operations  0.64 us (1%)
    pallas_call x1, Pallas kernels, per_device(): pl.pallas_call(body, out_shape=(jax.ShapeDtypeStruct((ROWS, C), BF16), ja...  52.7 us
    unnamed x1, local copies, waits for them, and re-layouts  2.06 us
    slice x1, local copies, waits for them, and re-layouts, per_device(): grad_conv = grad_conv[:, :KW * BLK].reshape(BLK, KW, BLK).transpose(2, 1, 0)  1.55 us

profile of v2, /device:TPU:1, one launch (start us, length us, event | category | flops | bytes accessed | tf_op | source)
XLA Modules:
  0.0 56.9 jit_solution(5211213767956514648)
XLA Ops:
  0.6 52.7 %shard_map.113 = (bf16[512,768]{1,0:T(8,128)(2,1)}, f32[48,256]{1,0:T(8,128)}) custom-call(bf16[512,768]{1,0:T(8,128)(2,1)} %bitcast.8, s32[1,512]{1,0:T(1,128)} %base_h.1, bf16[4,768]{1,0:T(4,128)(2,1)} %table_h.1, bf16[768]{0:T(1024)(128)(2,1)} %gain_h.1, bf16[5,768,768]{2,1,0:T(8,128)(2,1)} %wc_h.1, bf16[768,768]{1,0:T(8,128)(2,1)} %wq_h.1, ...), custom_call_target="tpu_custom_call" | custom-call | flops 1000000000 | bytes 12000000 | tf_op jit(solution)/shard_map/pallas_call | solution.py:480
  53.3 1.5 %copy.13 = f32[48,240]{0,1:T(8,128)} copy(f32[48,240]{1,0:T(8,128)} %bitcast.11) | data formatting | bytes 92160 | tf_op jit(solution)/shard_map/slice | solution.py:497
  54.9 2.1 %copy.15 = bf16[1,512,768]{2,1,0:T(8,128)(2,1)} copy(bf16[1,512,768]{2,1,0:T(8,128)(2,1)} %bitcast.7) | data formatting | bytes 1572864

commit v3 on v2

--- a/solution.py
+++ b/solution.py
@@ -21,6 +21,7 @@
 BLK = 48
 PARTS = 3
 SUB = 16
+COPIES = 4
 CHIPS = 16
 XW = 256
 EPSILON = 1e-06
@@ -31,6 +32,9 @@
 BF16 = jnp.bfloat16
 
 
+PLACE = (0, 2, 4, 8, 12, 14)
+
+
 def dot(a, b):
     return jnp.dot(a, b, preferred_element_type=F32)
 
@@ -48,10 +52,10 @@
 
 def body(
     feat_h, base_h, table_h, gain_h, wc_h, wq_h, wk_h, wv_h, wo_h, cot_h,
-    grad_in_ref, grad_conv_ref,
+    grad_in_h, grad_conv_ref,
     feat, base, table, gain, wc, wq, wk, wv, wo, cot,
     emb, act, normed, inv, slope, win, halo, xs, xr, xt,
-    qs, hb, pt, gst, go, gb, perm, grp, grr, grh, grs, rs, rr, edge,
+    qs, hb, pt, gst, go, gb, perm, grp, grr, grh, grs, rs, rr, edge, grad_in_ref,
     in_sem, send_sem, recv_sem,
 ):
     dp = lax.axis_index("dp")
@@ -62,6 +66,9 @@
     core = ctx % 2
     chip = me // 2
     slot = core * CHIPS + chip
+    pair = ctx // 2
+    head = pair - pair // 4 - pair // 6
+    is_head = (core == 0) & (pair != 3) & (pair != 5)
 
     def plane_id(p):
         return {"dp": zz * 2 + p // CTX, "ctx": p % CTX}
@@ -120,7 +127,7 @@
 
     rows_forward(0)
     rows_forward(ROWS - POOL)
-    @pl.loop(1, ROWS // POOL // 2)
+    @pl.loop(1, ROWS // POOL // 2, unroll=3)
     def _(i):
         rows_forward(pl.multiple_of(i * POOL, POOL))
 
@@ -178,7 +185,7 @@
 
     act_sides = sides(act.at[pl.ds(0, 16), :], act.at[pl.ds(ROWS - 16, 16), :], halo, 0)
 
-    @pl.loop(ROWS // POOL // 2, ROWS // POOL - 1)
+    @pl.loop(ROWS // POOL // 2, ROWS // POOL - 1, unroll=3)
     def _(i):
         rows_forward(pl.multiple_of(i * POOL, POOL))
 
@@ -192,6 +199,21 @@
     grad_attn = dot_rt(cot[...], wo[...]).astype(BF16)
     for h in range(HEADS):
         qs[h, 3] = grad_attn[:, h * DH : (h + 1) * DH]
+
+    def to_head(h, k):
+        return pltpu.make_async_remote_copy(
+            src_ref=qs.at[h, k], dst_ref=hb.at[k, pl.ds(pl.multiple_of(ctx * TOK, TOK), TOK), :],
+            send_sem=send_sem.at[4 + k], recv_sem=recv_sem.at[14 + k],
+            device_id={"dp": dp, "ctx": PLACE[h]}, device_id_type=MESH,
+        )
+
+    def to_heads(k):
+        for h in range(HEADS):
+            @pl.when(ctx != PLACE[h])
+            def _():
+                to_head(h, k).start()
+
+    to_heads(3)
 
     sides_arrive(act_sides)
     edge_win = jnp.concatenate([window_matrix(-16, 16), window_matrix(ROWS, 16)], axis=1)
@@ -225,48 +247,41 @@
 
     for i in range(7, 10):
         loads[i].wait()
-    for k, weight in enumerate((wq, wk, wv)):
+    for k, weight in ((1, wk), (0, wq), (2, wv)):
         made = dot(pooled, weight[...]).astype(BF16)
         for h in range(HEADS):
             qs[h, k] = made[:, h * DH : (h + 1) * DH]
-
-    def to_head(h):
+        to_heads(k)
+
+    @pl.loop(0, CTX)
+    def _(i):
+        x_send(other, (ctx + i) % CTX).start()
+
+    xr[slot] = xs[ctx]
+
+    def from_head(c, k):
         return pltpu.make_async_remote_copy(
-            src_ref=qs.at[h], dst_ref=hb.at[:, pl.ds(pl.multiple_of(ctx * TOK, TOK), TOK), :],
-            send_sem=send_sem.at[4 + h], recv_sem=recv_sem.at[4],
-            device_id={"dp": dp, "ctx": 2 * h}, device_id_type=MESH,
-        )
-
-    for h in range(HEADS):
-        @pl.when(ctx != 2 * h)
-        def _():
-            to_head(h).start()
-
-    @pl.loop(0, CTX)
-    def _(i):
-        x_send(other, (ctx + i) % CTX).start()
-
-    xr[slot] = xs[ctx]
-
-    head = ctx // 2
-    is_head = (ctx % 2 == 0) & (ctx < 2 * HEADS)
-
-    def from_head(c):
-        return pltpu.make_async_remote_copy(
-            src_ref=go.at[c], dst_ref=gb.at[head],
+            src_ref=go.at[c, k], dst_ref=gb.at[head, k],
             send_sem=send_sem.at[11], recv_sem=recv_sem.at[6],
             device_id={"dp": dp, "ctx": c}, device_id_type=MESH,
         )
+
+    def from_heads(k):
+        @pl.loop(1, CTX)
+        def _(i):
+            from_head((ctx + i) % CTX, k).start()
 
     @pl.when(is_head)
     def _():
         hb[:, pl.ds(pl.multiple_of(ctx * TOK, TOK), TOK), :] = qs[head]
-        arrived = hb.at[:, pl.ds(0, SEG_TOK - TOK), :]
-        pltpu.make_async_copy(arrived, arrived, recv_sem.at[4]).wait()
+        for k in range(4):
+            arrived = hb.at[k, pl.ds(0, SEG_TOK - TOK), :]
+            pltpu.make_async_copy(arrived, arrived, recv_sem.at[14 + k]).wait()
         scale = 1.0 / DH**0.5
         keys = hb[1]
         values = hb[2]
         values_t = values.T
+        keys_t = keys.T
 
         @pl.loop(0, SEG_TOK // 128)
         def _(i):
@@ -281,16 +296,19 @@
             delta = jnp.sum(grad.T.astype(F32) * out_t, axis=0, keepdims=True)
             grad_prob = dot_rt(values, grad)
             pt[:, part] = prob_b
-            gst[:, part] = (prob * (grad_prob - delta) * scale).astype(BF16)
-
-        go[:, 0] = dot(keys.T, gst[...]).T.astype(BF16).reshape(CTX, TOK, DH)
+            grad_score = (prob * (grad_prob - delta) * scale).astype(BF16)
+            gst[:, part] = grad_score
+            grad_query = dot(keys_t, grad_score).T.astype(BF16).reshape(4, TOK, DH)
+            for m in range(4):
+                go[4 * i + m, 0] = grad_query[m]
+                @pl.when(ctx != 4 * i + m)
+                def _():
+                    from_head(4 * i + m, 0).start()
+
+        go[:, 2] = dot(pt[...], hb[3]).astype(BF16).reshape(CTX, TOK, DH)
+        from_heads(2)
         go[:, 1] = dot(gst[...], hb[0]).astype(BF16).reshape(CTX, TOK, DH)
-        go[:, 2] = dot(pt[...], hb[3]).astype(BF16).reshape(CTX, TOK, DH)
-
-        @pl.loop(1, CTX)
-        def _(i):
-            from_head((ctx + i) % CTX).start()
-
+        from_heads(1)
         gb[head] = go[ctx]
         five = gb.at[pl.ds(0, HEADS - 1)]
         pltpu.make_async_copy(five, five, recv_sem.at[6]).wait()
@@ -324,7 +342,7 @@
 
     row_sides = sides(grs.at[pl.ds(0, 16), :], grs.at[pl.ds(16, 16), :], grh, 2)
 
-    @pl.loop(0, ROWS // POOL)
+    @pl.loop(0, ROWS // POOL, unroll=2)
     def _(i):
         rows = pl.ds(pl.multiple_of(i * POOL, POOL), POOL)
         u = normed[rows, :] * gain_f
@@ -400,7 +418,7 @@
 
     in_group = lax.broadcasted_iota(jnp.int32, (POOL, C), 0)
 
-    @pl.loop(0, TOK)
+    @pl.loop(0, TOK, unroll=2)
     def _(i):
         rows = pl.ds(pl.multiple_of(i * POOL, POOL), POOL)
         one = pl.ds(i, 1)
@@ -412,19 +430,31 @@
         mean = jnp.mean(g * n, axis=-1, keepdims=True)
         grad_in_ref[rows, :] = (edge[5, one, :] + inv[rows, :] * (g - n * mean)).astype(BF16)
 
+    grad_in_out = pltpu.make_async_copy(grad_in_ref, grad_in_h, in_sem.at[10])
+    grad_in_out.start()
+
     others = rr.at[pl.ds(0, NZ - 1)]
     pltpu.make_async_copy(others, others, recv_sem.at[10]).wait()
     total = rr[0].astype(F32)
     for z in range(1, NZ):
         total = total + rr[z].astype(F32)
-    grad_conv_ref[...] = total.reshape(BLK, XW)
-
+    total = jnp.concatenate([total.reshape(BLK, XW), jnp.zeros((128 - BLK, XW), F32)], axis=0).T
+    for j in range(KW):
+        grad_conv_ref[j] = total[j * BLK : (j + 1) * BLK, :BLK]
+
+    grad_in_out.wait()
     sides_sent(act_sides)
     sides_sent(row_sides)
-    for h in range(HEADS):
-        @pl.when(ctx != 2 * h)
-        def _():
-            to_head(h).wait_send()
+    for k in range(4):
+        @pl.when(is_head)
+        def _():
+            part = qs.at[pl.ds(0, HEADS - 1), k]
+            pltpu.make_async_copy(part, part, send_sem.at[4 + k]).wait()
+
+        @pl.when(jnp.logical_not(is_head))
+        def _():
+            part = qs.at[:, k]
+            pltpu.make_async_copy(part, part, send_sem.at[4 + k]).wait()
     part = xr.at[pl.ds(0, PLANE - 1)]
     pltpu.make_async_copy(part, part, send_sem.at[10]).wait()
 
@@ -439,6 +469,31 @@
         pass_on(k).wait_send()
     part = rr.at[pl.ds(0, NZ - 1)]
     pltpu.make_async_copy(part, part, send_sem.at[13]).wait()
+
+
+def write_out(grad_in_h, grad_conv_h, grad_in_o, grad_conv_o, rows_v, conv_v, in_sem, out_sem):
+    step = ROWS // COPIES
+    pieces = [pl.ds(i * step, step) for i in range(COPIES)]
+    steps = [
+        (
+            pltpu.make_async_copy(grad_in_h.at[rows, :], rows_v.at[rows, :], in_sem.at[i]),
+            pltpu.make_async_copy(rows_v.at[rows, :], grad_in_o.at[rows, :], out_sem.at[i]),
+        )
+        for i, rows in enumerate(pieces)
+    ]
+    steps.append(
+        (
+            pltpu.make_async_copy(grad_conv_h, conv_v, in_sem.at[COPIES]),
+            pltpu.make_async_copy(conv_v, grad_conv_o, out_sem.at[COPIES]),
+        )
+    )
+    for load, _ in steps:
+        load.start()
+    for load, store in steps:
+        load.wait()
+        store.start()
+    for _, store in steps:
+        store.wait()
 
 
 def per_device(
@@ -473,18 +528,19 @@
         vmem((PARTS, 128, XW), BF16),
         vmem((NZ, PARTS, SUB, XW), BF16),
         vmem((6, TOK, C), F32),
-        pltpu.SemaphoreType.DMA((10,)),
+        vmem((ROWS, C), BF16),
+        pltpu.SemaphoreType.DMA((11,)),
         pltpu.SemaphoreType.DMA((17,)),
-        pltpu.SemaphoreType.DMA((14,)),
+        pltpu.SemaphoreType.DMA((18,)),
     ]
     grad_in, grad_conv = pl.pallas_call(
         body,
         out_shape=(
             jax.ShapeDtypeStruct((ROWS, C), BF16),
-            jax.ShapeDtypeStruct((BLK, XW), F32),
+            jax.ShapeDtypeStruct((KW, BLK, BLK), F32),
         ),
         in_specs=[pl.BlockSpec(memory_space=pltpu.HBM)] * 10,
-        out_specs=(pl.BlockSpec(memory_space=pltpu.VMEM),) * 2,
+        out_specs=(pl.BlockSpec(memory_space=pltpu.HBM), pl.BlockSpec(memory_space=pltpu.VMEM)),
         scratch_shapes=scratch,
         compiler_params=pltpu.CompilerParams(
             collective_id=0, has_side_effects=True, vmem_limit_bytes=56 * 1024 * 1024
@@ -494,8 +550,21 @@
         features[0], bases, dna_table, norm_gain, w_conv, w_query, w_key, w_value, w_out,
         cotangent[0],
     )
-    grad_conv = grad_conv[:, : KW * BLK].reshape(BLK, KW, BLK).transpose(2, 1, 0)
-    return grad_in[None], grad_conv
+    grad_in, grad_conv = pl.pallas_call(
+        write_out,
+        out_shape=(
+            jax.ShapeDtypeStruct((ROWS, C), BF16),
+            jax.ShapeDtypeStruct((KW, BLK, BLK), F32),
+        ),
+        in_specs=[pl.BlockSpec(memory_space=pltpu.HBM)] * 2,
+        out_specs=(pl.BlockSpec(memory_space=pltpu.HBM),) * 2,
+        scratch_shapes=[
+            vmem((ROWS, C), BF16), vmem((KW, BLK, BLK), F32),
+            pltpu.SemaphoreType.DMA((COPIES + 1,)), pltpu.SemaphoreType.DMA((COPIES + 1,)),
+        ],
+        compiler_params=pltpu.CompilerParams(vmem_limit_bytes=56 * 1024 * 1024),
+    )(grad_in, grad_conv)
+    return grad_in[None], grad_conv.transpose(1, 0, 2)
 
 
 def solution(mesh):

time: 57.1 us -> 53.8 us (0.942)
  local copies, waits for them, and re-layouts: 3.61 us -> 0 us
    unnamed x1 -> x0, local copies, waits for them, and re-layouts: 2.06 us -> none
    pallas_call x0 -> x1, Pallas kernels: none -> 2.02 us  [per_device(): pl.pallas_call(write_out, out_shape=(jax.ShapeDtypeStruct((ROWS, C), BF16...]
    pallas_call x1, Pallas kernels: 52.7 us -> 51 us  [per_device(): pl.pallas_call(body, out_shape=(jax.ShapeDtypeStruct((ROWS, C), BF16), ja...]
    slice x1 -> x0, local copies, waits for them, and re-layouts: 1.55 us -> none  [per_device(): grad_conv = grad_conv[:, :KW * BLK].reshape(BLK, KW, BLK).transpose(2, 1, 0)]
where the time goes in v3:
time: 53.8 us; the launch traced here: 53.6 us
  Pallas kernels  53 us (99%)
  between operations  0.64 us (1%)
    pallas_call x1, Pallas kernels, per_device(): pl.pallas_call(body, out_shape=(jax.ShapeDtypeStruct((ROWS, C), BF16), ja...  51 us
    pallas_call x1, Pallas kernels, per_device(): pl.pallas_call(write_out, out_shape=(jax.ShapeDtypeStruct((ROWS, C), BF16...  2.02 us

profile of v3, /device:TPU:1, one launch (start us, length us, event | category | flops | bytes accessed | tf_op | source)
XLA Modules:
  0.0 53.6 jit_solution(16030787969221189947)
XLA Ops:
  0.6 51.0 %shard_map.113 = (bf16[512,768]{1,0:T(8,128)(2,1)}, f32[5,48,48]{2,1,0:T(8,128)}) custom-call(bf16[512,768]{1,0:T(8,128)(2,1)} %bitcast.4, s32[1,512]{1,0:T(1,128)} %base_h.1, bf16[4,768]{1,0:T(4,128)(2,1)} %table_h.1, bf16[768]{0:T(1024)(128)(2,1)} %gain_h.1, bf16[5,768,768]{2,1,0:T(8,128)(2,1)} %wc_h.1, bf16[768,768]{1,0:T(8,128)(2,1)} %wq_h.1, ...), custom_call_target="tpu_custom_call" | custom-call | flops 1000000000 | bytes 12000000 | tf_op jit(solution)/shard_map/pallas_call | solution.py:536
  51.6 2.0 %shard_map.114 = (bf16[512,768]{1,0:T(8,128)(2,1)}, f32[5,48,48]{2,1,0:T(8,128)}) custom-call(bf16[512,768]{1,0:T(8,128)(2,1)} %get-tuple-element.6.grad_in_h, f32[5,48,48]{2,1,0:T(8,128)} %get-tuple-element.7.grad_conv_h), custom_call_target="tpu_custom_call" | custom-call | tf_op jit(solution)/shard_map/pallas_call | solution.py:553

commit v4 on v3

--- a/solution.py
+++ b/solution.py
@@ -253,11 +253,23 @@
             qs[h, k] = made[:, h * DH : (h + 1) * DH]
         to_heads(k)
 
-    @pl.loop(0, CTX)
-    def _(i):
-        x_send(other, (ctx + i) % CTX).start()
-
-    xr[slot] = xs[ctx]
+    def to_other_half():
+        @pl.loop(0, CTX)
+        def _(i):
+            x_send(other, (ctx + i) % CTX).start()
+
+        xr[slot] = xs[ctx]
+
+    def slopes():
+        @pl.loop(0, ROWS // POOL, unroll=2)
+        def _(i):
+            rows = pl.ds(pl.multiple_of(i * POOL, POOL), POOL)
+            u = normed[rows, :] * gain_f
+            square = u * u
+            t = jnp.tanh(GELU_SCALE * (u + CUBIC * (square * u)))
+            d = 0.5 * (1.0 + t)
+            d = d + 0.5 * u * (1.0 - t * t) * GELU_SCALE * (1.0 + 3.0 * CUBIC * square)
+            slope[rows, :] = d * gain_f
 
     def from_head(c, k):
         return pltpu.make_async_remote_copy(
@@ -309,12 +321,15 @@
         from_heads(2)
         go[:, 1] = dot(gst[...], hb[0]).astype(BF16).reshape(CTX, TOK, DH)
         from_heads(1)
+        to_other_half()
         gb[head] = go[ctx]
         five = gb.at[pl.ds(0, HEADS - 1)]
         pltpu.make_async_copy(five, five, recv_sem.at[6]).wait()
 
     @pl.when(jnp.logical_not(is_head))
     def _():
+        slopes()
+        to_other_half()
         pltpu.make_async_copy(gb, gb, recv_sem.at[6]).wait()
 
     grad_pooled = cot[...].astype(F32)
@@ -342,14 +357,9 @@
 
     row_sides = sides(grs.at[pl.ds(0, 16), :], grs.at[pl.ds(16, 16), :], grh, 2)
 
-    @pl.loop(0, ROWS // POOL, unroll=2)
-    def _(i):
-        rows = pl.ds(pl.multiple_of(i * POOL, POOL), POOL)
-        u = normed[rows, :] * gain_f
-        square = u * u
-        t = jnp.tanh(GELU_SCALE * (u + CUBIC * (square * u)))
-        d = 0.5 * (1.0 + t) + 0.5 * u * (1.0 - t * t) * GELU_SCALE * (1.0 + 3.0 * CUBIC * square)
-        slope[rows, :] = d * gain_f
+    @pl.when(is_head)
+    def _():
+        slopes()
 
     others = xr.at[pl.ds(0, PLANE - 1)]
     pltpu.make_async_copy(others, others, recv_sem.at[5]).wait()

time: 53.8 us -> 52.2 us (0.970)
  Pallas kernels: 53 us -> 51.5 us
    pallas_call x1, Pallas kernels: 51 us -> 49.5 us  [per_device(): pl.pallas_call(body, out_shape=(jax.ShapeDtypeStruct((ROWS, C), BF16), ja...]
where the time goes in v4:
time: 52.2 us; the launch traced here: 52.1 us
  Pallas kernels  51.5 us (99%)
  between operations  0.64 us (1%)
    pallas_call x1, Pallas kernels, per_device(): pl.pallas_call(body, out_shape=(jax.ShapeDtypeStruct((ROWS, C), BF16), ja...  49.5 us
    pallas_call x1, Pallas kernels, per_device(): pl.pallas_call(write_out, out_shape=(jax.ShapeDtypeStruct((ROWS, C), BF16...  2.02 us

profile of v4, /device:TPU:1, one launch (start us, length us, event | category | flops | bytes accessed | tf_op | source)
XLA Modules:
  0.0 52.1 jit_solution(4854549805566368184)
XLA Ops:
  0.6 49.5 %shard_map.113 = (bf16[512,768]{1,0:T(8,128)(2,1)}, f32[5,48,48]{2,1,0:T(8,128)}) custom-call(bf16[512,768]{1,0:T(8,128)(2,1)} %bitcast.4, s32[1,512]{1,0:T(1,128)} %base_h.1, bf16[4,768]{1,0:T(4,128)(2,1)} %table_h.1, bf16[768]{0:T(1024)(128)(2,1)} %gain_h.1, bf16[5,768,768]{2,1,0:T(8,128)(2,1)} %wc_h.1, bf16[768,768]{1,0:T(8,128)(2,1)} %wq_h.1, ...), custom_call_target="tpu_custom_call" | custom-call | flops 1000000000 | bytes 12000000 | tf_op jit(solution)/shard_map/pallas_call | solution.py:546
  50.1 2.0 %shard_map.114 = (bf16[512,768]{1,0:T(8,128)(2,1)}, f32[5,48,48]{2,1,0:T(8,128)}) custom-call(bf16[512,768]{1,0:T(8,128)(2,1)} %get-tuple-element.6.grad_in_h, f32[5,48,48]{2,1,0:T(8,128)} %get-tuple-element.7.grad_conv_h), custom_call_target="tpu_custom_call" | custom-call | tf_op jit(solution)/shard_map/pallas_call | solution.py:563

commit v5 on v4

--- a/solution.py
+++ b/solution.py
@@ -21,7 +21,7 @@
 BLK = 48
 PARTS = 3
 SUB = 16
-COPIES = 4
+COPIES = 2
 CHIPS = 16
 XW = 256
 EPSILON = 1e-06
@@ -33,6 +33,12 @@
 
 
 PLACE = (0, 2, 4, 8, 12, 14)
+
+
+FAR_FIRST = sorted(
+    [(dx, dy) for dx in range(4) for dy in range(4) if dx or dy],
+    key=lambda d: -(min(d[0], 4 - d[0]) + min(d[1], 4 - d[1])),
+)
 
 
 def dot(a, b):
@@ -222,9 +228,9 @@
     low_part = (sums - high_part.astype(F32)).astype(BF16)
 
     for c in range(CTX):
-        cols = [sums[j * TOK : (j + 1) * TOK, c * BLK : (c + 1) * BLK] for j in range(KW)]
-        cols.append(jnp.zeros((TOK, XW - KW * BLK), F32))
-        xs[c] = jnp.concatenate(cols, axis=1).astype(BF16)
+        cols = [high_part[j * TOK : (j + 1) * TOK, c * BLK : (c + 1) * BLK] for j in range(KW)]
+        cols.append(jnp.zeros((TOK, XW - KW * BLK), BF16))
+        xs[c] = jnp.concatenate(cols, axis=1)
 
     other = 1 - hi
 
@@ -344,9 +350,8 @@
             grp[k, h] = sorted_g[:, first : first + 128]
 
     for k in range(PARTS):
-        @pl.loop(1, CHIPS)
-        def _(i):
-            to = (chip + i) % CHIPS
+        for dx, dy in FAR_FIRST:
+            to = (chip // 4 + dx) % 4 * 4 + (chip + dy) % 4
             pltpu.make_async_remote_copy(
                 src_ref=grp.at[k, to // (CHIPS // 2)], dst_ref=grr.at[k, slot],
                 send_sem=send_sem.at[12], recv_sem=recv_sem.at[7 + k],
@@ -386,8 +391,7 @@
         made = dot(xt[...], grr[k].reshape(PLANE * TOK, 128)) * factor
         rs[k] = made.T.astype(BF16)
 
-        @pl.loop(1, NZ)
-        def _(i):
+        for i in (4, 3, 5, 2, 6, 1, 7):
             z = (zz + i) % NZ
             pltpu.make_async_remote_copy(
                 src_ref=rs.at[k, pl.ds(pl.multiple_of(z * SUB, SUB), SUB), :], dst_ref=rr.at[zz, k],

time: 52.2 us -> 51.9 us (level)
  no operation moved by 1% of the time
where the time goes in v5:
time: 51.9 us; the launch traced here: 51.8 us
  Pallas kernels  51.1 us (98%)
  between operations  0.64 us (1%)
    pallas_call x1, Pallas kernels, per_device(): pl.pallas_call(body, out_shape=(jax.ShapeDtypeStruct((ROWS, C), BF16), ja...  49.2 us
    pallas_call x1, Pallas kernels, per_device(): pl.pallas_call(write_out, out_shape=(jax.ShapeDtypeStruct((ROWS, C), BF16...  1.95 us

profile of v5, /device:TPU:1, one launch (start us, length us, event | category | flops | bytes accessed | tf_op | source)
XLA Modules:
  0.0 51.8 jit_solution(258045828040440015)
XLA Ops:
  0.6 49.2 %shard_map.113 = (bf16[512,768]{1,0:T(8,128)(2,1)}, f32[5,48,48]{2,1,0:T(8,128)}) custom-call(bf16[512,768]{1,0:T(8,128)(2,1)} %bitcast.4, s32[1,512]{1,0:T(1,128)} %base_h.1, bf16[4,768]{1,0:T(4,128)(2,1)} %table_h.1, bf16[768]{0:T(1024)(128)(2,1)} %gain_h.1, bf16[5,768,768]{2,1,0:T(8,128)(2,1)} %wc_h.1, bf16[768,768]{1,0:T(8,128)(2,1)} %wq_h.1, ...), custom_call_target="tpu_custom_call" | custom-call | flops 1000000000 | bytes 12000000 | tf_op jit(solution)/shard_map/pallas_call | solution.py:550
  49.8 2.0 %shard_map.114 = (bf16[512,768]{1,0:T(8,128)(2,1)}, f32[5,48,48]{2,1,0:T(8,128)}) custom-call(bf16[512,768]{1,0:T(8,128)(2,1)} %get-tuple-element.6.grad_in_h, f32[5,48,48]{2,1,0:T(8,128)} %get-tuple-element.7.grad_conv_h), custom_call_target="tpu_custom_call" | custom-call | tf_op jit(solution)/shard_map/pallas_call | solution.py:567

commit v6 on v5

--- a/solution.py
+++ b/solution.py
@@ -40,6 +40,11 @@
     key=lambda d: -(min(d[0], 4 - d[0]) + min(d[1], 4 - d[1])),
 )
 
+SEGMENT_FAR_FIRST = sorted(
+    [(dx, dy, dc) for dx in range(2) for dy in range(4) for dc in range(2) if dx or dy or dc],
+    key=lambda d: -(d[0] + min(d[1], 4 - d[1])),
+)
+
 
 def dot(a, b):
     return jnp.dot(a, b, preferred_element_type=F32)
@@ -285,9 +290,9 @@
         )
 
     def from_heads(k):
-        @pl.loop(1, CTX)
-        def _(i):
-            from_head((ctx + i) % CTX, k).start()
+        for dx, dy, dc in SEGMENT_FAR_FIRST:
+            row = (pair // 4 + dx) % 2 * 4 + (pair + dy) % 4
+            from_head(2 * row + (core + dc) % 2, k).start()
 
     @pl.when(is_head)
     def _():

time: 51.9 us -> 51.4 us (level)
  no operation moved by 1% of the time
where the time goes in v6:
time: 51.4 us; the launch traced here: 51.3 us
  Pallas kernels  50.6 us (98%)
  between operations  0.64 us (1%)
    pallas_call x1, Pallas kernels, per_device(): pl.pallas_call(body, out_shape=(jax.ShapeDtypeStruct((ROWS, C), BF16), ja...  48.7 us
    pallas_call x1, Pallas kernels, per_device(): pl.pallas_call(write_out, out_shape=(jax.ShapeDtypeStruct((ROWS, C), BF16...  1.95 us

profile of v6, /device:TPU:1, one launch (start us, length us, event | category | flops | bytes accessed | tf_op | source)
XLA Modules:
  0.0 51.3 jit_solution(14749317980634491926)
XLA Ops:
  0.6 48.7 %shard_map.113 = (bf16[512,768]{1,0:T(8,128)(2,1)}, f32[5,48,48]{2,1,0:T(8,128)}) custom-call(bf16[512,768]{1,0:T(8,128)(2,1)} %bitcast.4, s32[1,512]{1,0:T(1,128)} %base_h.1, bf16[4,768]{1,0:T(4,128)(2,1)} %table_h.1, bf16[768]{0:T(1024)(128)(2,1)} %gain_h.1, bf16[5,768,768]{2,1,0:T(8,128)(2,1)} %wc_h.1, bf16[768,768]{1,0:T(8,128)(2,1)} %wq_h.1, ...), custom_call_target="tpu_custom_call" | custom-call | flops 1000000000 | bytes 12000000 | tf_op jit(solution)/shard_map/pallas_call | solution.py:555
  49.3 2.0 %shard_map.114 = (bf16[512,768]{1,0:T(8,128)(2,1)}, f32[5,48,48]{2,1,0:T(8,128)}) custom-call(bf16[512,768]{1,0:T(8,128)(2,1)} %get-tuple-element.6.grad_in_h, f32[5,48,48]{2,1,0:T(8,128)} %get-tuple-element.7.grad_conv_h), custom_call_target="tpu_custom_call" | custom-call | tf_op jit(solution)/shard_map/pallas_call | solution.py:572
